TPU v7x, 512 devices: a whole 4x8x8 slice. The times are simulated.
512 devices in a mesh: gx: 32 (over y, x), gy: 16 (over z, core).
Axes of the slice: x: 4, y: 8, z: 8, core: 2. Of those that a mesh axis runs over, the one named last changes fastest.
Arguments:
- residual_in: float32 [448, 224, 336], P('gx', 'gy'), may hold values from -8 to 8
Outputs:
- correction: float32 [448, 224, 336], P('gx', 'gy')
- coarse_correction: float32 [64, 32, 48], P('gx', 'gy')
All inputs are finite; a program needn't handle non-finite values.
Results may differ from a plain program's by a relative error of at most 0.0003.
Values sent between devices are 32-bit elements; how exact they have to be, the bound alone decides.
No kernel may reach another device: no remote copies, remote signals or barrier semaphores. Data moves between devices by JAX's collectives and lax.ppermute only.
A program may use at most 64 MiB of HBM per device.

v0:
```python
import math

import jax
import jax.numpy as jnp
import numpy as np
from jax import lax
from jax.sharding import PartitionSpec as P

spectral_radius_bound = lax.Precision.HIGHEST
theta_cheb = 1.125
delta_cheb = 0.875
start_points = [
    -0.8717401485096066,
    -0.5917001814331423,
    -0.2092992179024789,
    0.2092992179024789,
    0.5917001814331423,
    0.8717401485096066,
]


def extended_2(cells, sides, width):
    for axis, dim in sides:
        count = lax.axis_size(axis)
        ends = count - 1
        head = lax.slice_in_dim(cells, 0, width, axis=dim)
        tail = lax.slice_in_dim(cells, cells.shape[dim] - width, cells.shape[dim], axis=dim)
        cells = jnp.concatenate(
            [
                lax.ppermute(tail, axis, [(i, (i + 1) % count) for i in range(ends)]),
                cells,
                lax.ppermute(head, axis, [((i + 1) % count, i) for i in range(ends)]),
            ],
            axis=dim,
        )
    return cells


def from_behind(block, axis, distance):
    devices = range(lax.axis_size(axis))
    route = [(i - distance, i) for i in devices if i - distance in devices]
    return lax.ppermute(block, axis, route)


def legendre_pair(value):
    before, now = (1.0, value)
    for order in range(1, 7):
        before, now = (now, ((2 * order + 1) * value * now - order * before) / (order + 1))
    return (now, before)


def lobatto_tables():
    point_list = [-1.0]
    for guess in start_points:
        place = guess
        for newton in range(4):
            seventh, sixth = legendre_pair(place)
            slope = 7.0 * (place * seventh - sixth) / (place * place - 1.0)
            curve = (2.0 * place * slope - 56.0 * seventh) / (1.0 - place * place)
            place = place - slope / curve
        point_list.append(place)
    point_list.append(1.0)
    sample_nodes_list = np.array(point_list)
    values = np.array([legendre_pair(place)[0] for place in point_list])
    weights = 2.0 / (56.0 * values * values)
    derivative = np.zeros((8, 8))
    for i in range(8):
        for j in range(8):
            if i != j:
                derivative[i, j] = values[i] / (
                    values[j] * (sample_nodes_list[i] - sample_nodes_list[j])
                )
    derivative[0, 0] = -14.0
    derivative[7, 7] = 14.0
    stiffness = derivative.T @ (weights[:, None] * derivative)
    return (sample_nodes_list, weights, stiffness)


def assemble(elements, stiffness, weights):
    width = 7 * elements + 1
    assembled = np.zeros((width, width))
    masses = np.zeros(width)
    for e in range(elements):
        assembled[7 * e : 7 * e + 8, 7 * e : 7 * e + 8] += stiffness
        masses[7 * e : 7 * e + 8] += weights
    return (assembled, masses)


def jacobi_eigen(matrix):
    order = matrix.shape[0]
    work = [[float(matrix[i, j]) for j in range(order)] for i in range(order)]
    vectors = [[1.0 if i == j else 0.0 for j in range(order)] for i in range(order)]
    for sweep in range(12):
        for p in range(order):
            for q in range(p + 1, order):
                angle = 0.5 * math.atan2(2.0 * work[p][q], work[q][q] - work[p][p])
                cosine = math.cos(angle)
                sine = math.sin(angle)
                for k in range(order):
                    left, right = (work[k][p], work[k][q])
                    work[k][p] = cosine * left - sine * right
                    work[k][q] = sine * left + cosine * right
                for k in range(order):
                    left, right = (work[p][k], work[q][k])
                    work[p][k] = cosine * left - sine * right
                    work[q][k] = sine * left + cosine * right
                for k in range(order):
                    left, right = (vectors[k][p], vectors[k][q])
                    vectors[k][p] = cosine * left - sine * right
                    vectors[k][q] = sine * left + cosine * right
    return (np.array([work[i][i] for i in range(order)]), np.array(vectors))


def schwarz_basis():
    sample_nodes_list, weights, stiffness = lobatto_tables()
    assembled, masses = assemble(3, stiffness, weights)
    block_stiff = assembled[6:16, 6:16]
    inv_root = 1.0 / np.sqrt(masses[6:16])
    eigen_vals, eigen_vecs = jacobi_eigen(inv_root[:, None] * block_stiff * inv_root[None, :])
    return (inv_root[:, None] * eigen_vecs, eigen_vals)


def forward_table(elements, eigen_basis):
    matrix = np.zeros((10 * elements, 7 * elements + 4))
    for j in range(elements):
        matrix[10 * j : 10 * j + 10, 7 * j + 1 : 7 * j + 11] = eigen_basis.T
    return matrix


def backward_table(elements, eigen_basis):
    matrix = np.zeros((7 * elements, 10 * elements))
    for j in range(elements):
        matrix[7 * j : 7 * j + 7, 10 * j : 10 * j + 10] = eigen_basis[1:8]
    return matrix


def injection_coefficients(elements, sample_nodes_list):
    matrix = np.zeros((elements + 1, 7 * elements))
    for e in range(elements):
        for m in range(7):
            matrix[e, 7 * e + m] += (1.0 - sample_nodes_list[m]) / 2.0
            matrix[e + 1, 7 * e + m] += (1.0 + sample_nodes_list[m]) / 2.0
    return matrix


def sine_table(vertex, modes_in, elements):
    operator_output = vertex[:, None] * modes_in[None, :] % (2 * elements)
    angles = jnp.pi * modes_in.astype(jnp.float32) / elements
    entries = jnp.sqrt(2.0 / elements) * jnp.sin(
        jnp.pi * operator_output.astype(jnp.float32) / elements
    )
    entries = entries / jnp.sqrt((4.0 + 2.0 * jnp.cos(angles)) / 3.0)[None, :]
    return jnp.where(modes_in[None, :] > 0, entries, 0.0)


def coarse_eigen(modes_in, elements):
    angles = jnp.pi * modes_in.astype(jnp.float32) / elements
    return jnp.where(
        modes_in > 0, 3.0 * (1.0 - jnp.cos(angles)) / (4.0 + 2.0 * jnp.cos(angles)), 1.0
    )


def frozen_literal(matrix):
    return jnp.asarray(matrix, jnp.float32)


def rims(nodal):
    return extended_2(nodal, (("gx", 0), ("gy", 1)), 2)


def stiff_last(nodal, element_stiff):
    lead_a, lead_b, count_z = nodal.shape
    elements = count_z // 7
    blocks = nodal.reshape(lead_a, lead_b, elements, 7)
    next_nodes = jnp.concatenate(
        [nodal[:, :, 7::7], jnp.zeros((lead_a, lead_b, 1), nodal.dtype)], axis=2
    )
    stacked = jnp.concatenate([blocks, next_nodes[:, :, :, None]], axis=3)
    operator_output = jnp.einsum(
        "ij,abej->abei", element_stiff, stacked, precision=spectral_radius_bound
    )
    result = operator_output[:, :, :, :7]
    result = result.at[:, :, 1:, 0].add(operator_output[:, :, :-1, 7])
    return result.reshape(lead_a, lead_b, count_z)


def per_device(residual_in):
    sample_nodes_list, weights, stiffness = lobatto_tables()
    eigen_basis, eigen_vals = schwarz_basis()
    nodes_x, nodes_y, nodes_z = residual_in.shape
    cells_horizontal, elems_y, element_tally_along_height = (
        nodes_x // 7,
        nodes_y // 7,
        nodes_z // 7,
    )
    index_x = lax.axis_index("gx")
    vertical_position = lax.axis_index("gy")
    count_x = lax.axis_size("gx") * cells_horizontal
    count_y = lax.axis_size("gy") * elems_y
    interior = (
        (index_x * nodes_x + jnp.arange(nodes_x) > 0)[:, None, None]
        & (vertical_position * nodes_y + jnp.arange(nodes_y) > 0)[None, :, None]
        & (jnp.arange(nodes_z) > 0)[None, None, :]
    ).astype(jnp.float32)
    forward_x = frozen_literal(forward_table(cells_horizontal, eigen_basis))
    forward_y = frozen_literal(forward_table(elems_y, eigen_basis))
    backward_x = frozen_literal(backward_table(cells_horizontal, eigen_basis))
    backward_y = frozen_literal(backward_table(elems_y, eigen_basis))
    basis_small = frozen_literal(eigen_basis)
    kept_small = frozen_literal(eigen_basis[1:8])
    element_stiff = frozen_literal(stiffness)
    denominator = (
        frozen_literal(np.tile(eigen_vals, cells_horizontal))[:, None, None]
        + frozen_literal(np.tile(eigen_vals, elems_y))[None, :, None]
        + frozen_literal(np.tile(eigen_vals, element_tally_along_height))[None, None, :]
    )
    assembled_z, inertia_weights_height = assemble(element_tally_along_height, stiffness, weights)
    mass_z = frozen_literal(inertia_weights_height[:nodes_z])

    def smooth(nodal):
        extended = rims(nodal)
        coeffs = jnp.einsum("ap,pqz->aqz", forward_x, extended, precision=spectral_radius_bound)
        coeffs = jnp.einsum("bq,aqz->abz", forward_y, coeffs, precision=spectral_radius_bound)
        rows_a, rows_b = (coeffs.shape[0], coeffs.shape[1])
        padded = jnp.pad(coeffs, ((0, 0), (0, 0), (1, 6)))
        own_part = padded[:, :, :nodes_z].reshape(rows_a, rows_b, element_tally_along_height, 7)
        next_part = padded[:, :, 7 : nodes_z + 7].reshape(
            rows_a, rows_b, element_tally_along_height, 7
        )[:, :, :, :3]
        window = jnp.concatenate([own_part, next_part], axis=3)
        coeffs = jnp.einsum("abem,mc->abec", window, basis_small, precision=spectral_radius_bound)
        coeffs = coeffs.reshape(rows_a, rows_b, 10 * element_tally_along_height) / denominator
        coeffs = jnp.einsum(
            "abec,ic->abei",
            coeffs.reshape(rows_a, rows_b, element_tally_along_height, 10),
            kept_small,
            precision=spectral_radius_bound,
        )
        coeffs = coeffs.reshape(rows_a, rows_b, nodes_z)
        coeffs = jnp.einsum("qb,abz->aqz", backward_y, coeffs, precision=spectral_radius_bound)
        coeffs = jnp.einsum("pa,aqz->pqz", backward_x, coeffs, precision=spectral_radius_bound)
        return interior * coeffs

    def operate(nodal):
        local_x, local_mass_x = assemble(cells_horizontal, stiffness, weights)
        local_y, local_mass_y = assemble(elems_y, stiffness, weights)
        stiff_x = frozen_literal(local_x)
        stiff_y = frozen_literal(local_y)
        mass_x = frozen_literal(local_mass_x)
        mass_y = frozen_literal(local_mass_y)
        extended = rims(nodal)
        shared_rows = extended[2 : nodes_x + 3, 2 : nodes_y + 3]
        partial_value = jnp.einsum(
            "pa,aqz->pqz", stiff_x, shared_rows, precision=spectral_radius_bound
        )
        partial_value = partial_value * (mass_y[:, None] * mass_z[None, :])[None]
        across = jnp.einsum("qb,pbz->pqz", stiff_y, shared_rows, precision=spectral_radius_bound)
        partial_value = partial_value + mass_x[:, None, None] * across * mass_z[None, None, :]
        along = stiff_last(shared_rows, element_stiff)
        partial_value = partial_value + (mass_x[:, None] * mass_y[None, :])[:, :, None] * along
        from_below_x = from_behind(partial_value[nodes_x], "gx", 1)
        merged = partial_value[:nodes_x].at[0].add(from_below_x)
        from_below_y = from_behind(merged[:, nodes_y], "gy", 1)
        summed = merged[:, :nodes_y].at[:, 0].add(from_below_y)
        return interior * summed

    source = interior * residual_in
    sigma_ratio = theta_cheb / delta_cheb
    rho_now = 1.0 / sigma_ratio
    direction = smooth(source) / theta_cheb
    approx = direction
    remain = source - operate(direction)
    rho_next = 1.0 / (2.0 * sigma_ratio - rho_now)
    direction = rho_next * rho_now * direction + 2.0 * rho_next / delta_cheb * smooth(remain)
    approx = approx + direction
    remain = remain - operate(direction)
    restrict_x = frozen_literal(injection_coefficients(cells_horizontal, sample_nodes_list))
    restrict_y = frozen_literal(injection_coefficients(elems_y, sample_nodes_list))
    thinning_upright_map = frozen_literal(
        injection_coefficients(element_tally_along_height, sample_nodes_list)[
            :element_tally_along_height
        ]
    )
    local_coarse_portion = jnp.einsum(
        "ap,pqz->aqz", restrict_x, remain, precision=spectral_radius_bound
    )
    local_coarse_portion = jnp.einsum(
        "bq,aqz->abz", restrict_y, local_coarse_portion, precision=spectral_radius_bound
    )
    local_coarse_portion = jnp.einsum(
        "abz,mz->abm", local_coarse_portion, thinning_upright_map, precision=spectral_radius_bound
    )
    vertex_x = index_x * cells_horizontal + jnp.arange(cells_horizontal + 1)
    vertex_y = vertical_position * elems_y + jnp.arange(elems_y + 1)
    phi_x = sine_table(vertex_x, jnp.arange(count_x), count_x)
    phi_y = sine_table(vertex_y, jnp.arange(count_y), count_y)
    basis_functions_depth = sine_table(
        jnp.arange(element_tally_along_height),
        jnp.arange(element_tally_along_height),
        element_tally_along_height,
    )
    eigen_z = coarse_eigen(jnp.arange(element_tally_along_height), element_tally_along_height)
    third_axis_direction = jnp.einsum(
        "ocg,gw->ocw", local_coarse_portion, basis_functions_depth, precision=spectral_radius_bound
    )
    mode_rows = cells_horizontal * elems_y
    half_modes = jnp.einsum(
        "pqk,qb->pbk", third_axis_direction, phi_y, precision=spectral_radius_bound
    )
    all_modes = jnp.einsum("pa,pbk->abk", phi_x, half_modes, precision=spectral_radius_bound)
    all_modes = all_modes.reshape(count_x * count_y, element_tally_along_height)
    mode_eigenvalues = lax.psum_scatter(all_modes, ("gx", "gy"), scatter_dimension=0, tiled=True)
    first_row = (index_x * lax.axis_size("gy") + vertical_position) * mode_rows
    mode_index = first_row + jnp.arange(mode_rows)
    scaled = mode_eigenvalues / (
        coarse_eigen(mode_index // count_y, count_x)[:, None]
        + coarse_eigen(mode_index % count_y, count_y)[:, None]
        + eigen_z[None, :]
    )
    gathered_piece = lax.all_gather(scaled, ("gx", "gy"), axis=0, tiled=True)
    mode_index = jnp.arange(gathered_piece.shape[0])
    first_axis_table = sine_table(vertex_x, mode_index // count_y, count_x)
    table_y = sine_table(vertex_y, mode_index % count_y, count_y)
    collected_values = jnp.einsum(
        "pr,qr,rk->pqk", first_axis_table, table_y, gathered_piece, precision=spectral_radius_bound
    )
    crude_mesh_entries = jnp.einsum(
        "lyn,fn->lyf", collected_values, basis_functions_depth, precision=spectral_radius_bound
    )
    fine_level_portion = jnp.einsum(
        "pgh,hi->pgi", crude_mesh_entries, thinning_upright_map, precision=spectral_radius_bound
    )
    fine_level_portion = jnp.einsum(
        "bq,pbz->pqz", restrict_y, fine_level_portion, precision=spectral_radius_bound
    )
    fine_level_portion = jnp.einsum(
        "ap,aqz->pqz", restrict_x, fine_level_portion, precision=spectral_radius_bound
    )
    correction = approx + interior * fine_level_portion
    return (correction, crude_mesh_entries[:cells_horizontal, :elems_y, :])


def solution(mesh):
    return jax.shard_map(
        per_device,
        mesh=mesh,
        in_specs=(P("gx", "gy", None),),
        out_specs=(P("gx", "gy", None), P("gx", "gy", None)),
        check_vma=False,
    )
```

profile of v0, /device:TPU:1, one launch (start us, length us, event | category | flops | bytes accessed | tf_op | source)
XLA Modules:
  0.0 674.4 jit_solution(3499132589935595326)
XLA Ops:
  8.5 3.9 collective-permute-start
  17.2 6.0 collective-permute-start.2
  45.7 3.1 copy.122
  48.8 4.0 fusion
  52.8 2.7 fusion.8
  55.6 2.8 copy.123
  58.4 3.1 reshape.592
  61.5 4.0 convolution_bitcast_fusion.3
  66.8 3.1 collective-permute-start.4
  71.9 2.8 collective-permute-done.5
  77.3 3.2 collective-permute-done.6
  86.4 3.3 fusion.25
  91.6 38.5 %scatter-add.20 = f32[15,15,48,7]{2,3,1,0:T(8,128)} dynamic-update-slice(f32[15,15,48,7]{2,3,1,0:T(8,128)} %bitcast.143, f32[15,15,47,1]{2,3,1,0:T(1,128)S(1)} %slice_add_fusion.1, s32[]{:T(128)} %constant.370.clone.1, s32[]{:T(128)} %constant.370.clone.1, s32[]{:T(128)} %constant.375.clone.1, s32[]{:T(128)} %constant.370.clone.1) | dynamic-update-slice | bytes 84604 | tf_op jit(solution)/shard_map/scatter-add | solution.py:183
  135.5 4.7 collective-permute-start.7
  146.6 4.6 collective-permute-start.9
  152.5 4.7 collective-permute-start.11
  159.8 3.2 collective-permute-done.12
  166.1 12.0 %copy.137 = f32[20,20,336]{1,2,0:T(8,128)S(1)} copy(f32[20,20,336]{2,1,0:T(8,128)} %get-tuple-element.83) | data formatting | bytes 1075200 | tf_op jit(solution)/shard_map/slice | solution.py:227
  188.2 3.1 copy.139
  191.3 4.0 fusion.4
  195.4 2.7 fusion.9
  198.1 2.8 copy.140
  200.9 2.9 reshape.599
  203.8 4.0 convolution_bitcast_fusion.2
  208.4 4.6 collective-permute-start.13
  214.9 3.5 collective-permute-done.14
  220.9 3.2 collective-permute-done.15
  232.9 3.2 fusion.29
  237.9 38.5 %scatter-add.25 = f32[15,15,48,7]{2,3,1,0:T(8,128)} dynamic-update-slice(f32[15,15,48,7]{2,3,1,0:T(8,128)} %bitcast.144, f32[15,15,47,1]{2,3,1,0:T(1,128)S(1)} %slice_add_fusion, s32[]{:T(128)} %constant.370.clone.1, s32[]{:T(128)} %constant.370.clone.1, s32[]{:T(128)} %constant.375.clone.1, s32[]{:T(128)} %constant.370.clone.1) | dynamic-update-slice | bytes 84604 | tf_op jit(solution)/shard_map/scatter-add | solution.py:183
  282.5 5.7 collective-permute-start.16
  298.9 290.6 %all-reduce.7.cloned.1.call-done = f32[2048,48]{0,1:T(8,128)} async-done(((f32[2048,48]{0,1:T(8,128)}), f32[2048,48]{0,1:T(8,128)}) %all-reduce.7.cloned.1.call-update) | async-done | bytes 393232
  590.4 73.2 %all-gather = f32[512,4,48]{2,1,0:T(4,128)S(1)} all-gather(f32[1,4,48]{2,1,0:T(4,128)S(1)} %copy.156), channel_id=1, replica_groups=mesh['gx'=32,'gy'=16] {'gx','gy'}, dimensions={0}, use_global_device_ids=true | all-gather | bytes 393984 | tf_op jit(solution)/shard_map/all_gather | solution.py:320
  (209 shorter events, 107.2 us)
Async XLA Ops:
  7.2 582.3 %all-reduce.7.cloned.1.call-start = ((), (), s32[]{:S(2)}) async-start(), calls=%async_computation | async-start | bytes 786432
  7.2 200.5 %copy-start.18 = (pred[336]{0:T(512)(128)(4,1)}, pred[336]{0:T(512)(128)(4,1)S(1)}, u32[]{:S(2)}) copy-start(pred[336]{0:T(512)(128)(4,1)S(1)} %iota_compare_fusion) | copy-start | bytes 1012
  8.5 8.7 %collective-permute-start = (f32[2,14,336]{2,0,1:T(2,128)S(1)}, f32[2,14,336]{2,0,1:T(2,128)S(1)}, u32[]{:S(2)}, u32[]{:S(2)}) collective-permute-start(f32[2,14,336]{2,0,1:T(2,128)S(1)} %get-tuple-element.100), channel_id=1, source_target_pairs={{0,16},{16,32},{32,48},{48,64},{64,80},{80,96},{96,112},{112,128},... | collective-permute-start | bytes 112904 | tf_op jit(solution)/shard_map/ppermute | solution.py:30
  12.4 4.8 collective-permute-start.1
  14.6 38.2 %copy-start.22 = (f32[20,20]{1,0:T(8,128)}, f32[20,20]{1,0:T(8,128)S(1)}, u32[]{:S(2)}) copy-start(f32[20,20]{1,0:T(8,128)S(1)} %broadcast_add_fusion) | copy-start | bytes 4804
  14.6 20.9 %copy-start.25 = (s32[3]{0:T(128)}, s32[3]{0:T(128)S(1)}, u32[]{:S(2)}) copy-start(s32[3]{0:T(128)S(1)} %iota_add_fusion) | copy-start | bytes 40
  15.4 118.7 %copy-start.7 = (f32[15,336]{1,0:T(8,128)}, f32[15,336]{1,0:T(8,128)S(1)}, u32[]{:S(2)}) copy-start(f32[15,336]{1,0:T(8,128)S(1)} %broadcast_multiply_fusion.1) | copy-start | bytes 60484
  17.1 117.0 %copy-start.12 = (f32[15,15]{1,0:T(8,128)}, f32[15,15]{1,0:T(8,128)S(1)}, u32[]{:S(2)}) copy-start(f32[15,15]{1,0:T(8,128)S(1)} %broadcast_multiply_fusion.2) | copy-start | bytes 2704
  17.2 9.2 %collective-permute-start.2 = (f32[18,2,336]{2,0,1:T(8,128)S(1)}, f32[18,2,336]{2,0,1:T(8,128)S(1)}, u32[]{:S(2)}, u32[]{:S(2)}) collective-permute-start(f32[18,2,336]{2,0,1:T(8,128)S(1)} %get-tuple-element.88), channel_id=1, source_target_pairs={{0,1},{1,2},{2,3},{3,4},{4,5},{5,6},{6,7},{7,8},{8,9},{9,10},{10,1... | collective-permute-start | bytes 145160 | tf_op jit(solution)/shard_map/ppermute | solution.py:30
  23.2 5.7 collective-permute-start.3
  66.8 5.1 collective-permute-start.4
  70.0 4.8 collective-permute-start.5
  74.7 5.7 collective-permute-start.6
  133.6 29.3 %copy-start.13 = (f32[20,18,1]{1,0,2:T(8,128)S(1)}, f32[20,18,1]{1,0,2:T(8,128)}, u32[]{:S(2)}) copy-start(f32[20,18,1]{1,0,2:T(8,128)} %constant.426) | copy-start | bytes 4324
  135.5 5.6 collective-permute-start.7
  140.2 24.2 %copy-start.27 = (s32[3]{0:T(128)}, s32[3]{0:T(128)S(1)}, u32[]{:S(2)}) copy-start(s32[3]{0:T(128)S(1)} %iota_add_fusion.1) | copy-start | bytes 40
  141.3 3.7 collective-permute-start.8
  145.2 17.7 %copy-start = (f32[14,14,336]{2,0,1:T(8,128)}, f32[14,14,336]{2,0,1:T(8,128)S(1)}, u32[]{:S(2)}) copy-start(f32[14,14,336]{2,0,1:T(8,128)S(1)} %fusion.59) | copy-start | bytes 790276
  145.3 6.5 collective-permute-start.10
  146.6 5.9 collective-permute-start.9
  152.5 7.2 %collective-permute-start.11 = (f32[18,2,336]{2,0,1:T(8,128)S(1)}, f32[18,2,336]{2,0,1:T(8,128)S(1)}, u32[]{:S(2)}, u32[]{:S(2)}) collective-permute-start(f32[18,2,336]{2,0,1:T(8,128)S(1)} %get-tuple-element.86), channel_id=1, source_target_pairs={{0,1},{1,2},{2,3},{3,4},{4,5},{5,6},{6,7},{7,8},{8,9},{9,10},{10,1... | collective-permute-start | bytes 145160 | tf_op jit(solution)/shard_map/ppermute | solution.py:30
  157.3 5.7 collective-permute-start.12
  208.4 6.5 collective-permute-start.13
  213.0 5.4 collective-permute-start.14
  218.4 5.7 collective-permute-start.15
  278.6 16.1 %copy-start.6 = (f32[48,336,1]{1,0,2:T(8,128)S(1)}, f32[48,336,1]{1,0,2:T(8,128)}, u32[]{:S(2)}) copy-start(f32[48,336,1]{1,0,2:T(8,128)} %constant.432) | copy-start | bytes 193540
  282.5 6.7 collective-permute-start.16
  289.2 3.6 collective-permute-start.17
  292.9 370.7 %copy-start.10 = (f32[2048,3]{0,1:T(4,128)S(1)}, f32[2048,3]{0,1:T(4,128)}, u32[]{:S(2)}) copy-start(f32[2048,3]{0,1:T(4,128)} %select_bitcast_fusion) | copy-start | bytes 73732
  292.9 370.7 %copy-start.11 = (f32[2048,3]{0,1:T(4,128)S(1)}, f32[2048,3]{0,1:T(4,128)}, u32[]{:S(2)}) copy-start(f32[2048,3]{0,1:T(4,128)} %select_bitcast_fusion.1) | copy-start | bytes 73732
  295.7 370.0 %copy-start.4 = (f32[14,14,336]{2,0,1:T(8,128)S(1)}, f32[14,14,336]{2,0,1:T(8,128)}, u32[]{:S(2)}) copy-start(f32[14,14,336]{2,0,1:T(8,128)} %get-tuple-element.103) | copy-start | bytes 790276
  295.7 370.0 %copy-start.19 = (pred[336]{0:T(512)(128)(4,1)S(1)}, pred[336]{0:T(512)(128)(4,1)}, u32[]{:S(2)}) copy-start(pred[336]{0:T(512)(128)(4,1)} %copy-done.18) | copy-start | bytes 1012
  (26 other events, 200.0 us)
Sparse Core Ops, SparseCore 0:
  298.9 290.5 all-reduce.6
where the time goes:
time: 684 us; the launch traced here: 674 us
  waiting for transfers between devices  312 us (46%)
  local copies, waits for them, and re-layouts  157 us (23%)
  blocking collectives  73.2 us (11%)
  starting transfers between devices  56.3 us (8%)
  matrix products  45 us (7%)
  between operations  15.6 us (2%)
  other arithmetic  14.8 us (2%)
    unnamed x2, waiting for transfers between devices  291 us
    scatter-add x4, local copies, waits for them, and re-layouts, stiff_last(): result = result.at[:, :, 1:, 0].add(operator_output[:, :, :-1, 7])  81.3 us
    all_gather x1, blocking collectives, per_device(): gathered_piece = lax.all_gather(scaled, ('gx', 'gy'), axis=0, tiled=True)  73.2 us
    ppermute x6, starting transfers between devices, extended_2(): lax.ppermute(tail, axis, [(i, (i + 1) % count) for i in range(ends)])  27 us
    ppermute x8, waiting for transfers between devices, extended_2(): lax.ppermute(head, axis, [((i + 1) % count, i) for i in range(ends)])  18.3 us
    slice x6, local copies, waits for them, and re-layouts, smooth(): padded[:, :, 7:nodes_z + 7]  16.8 us
    ppermute x4, starting transfers between devices, from_behind(): return lax.ppermute(block, axis, route)  15.8 us
  transfers between devices with their start and end apart: 19, of which 12 were waited for; matrix products, arithmetic and copies ran while one was open for 1% of the time, Pallas kernels for 0%

commit v1 on v0

v1 whole, which is shorter than its diff:
```python
import math

import jax
import jax.numpy as jnp
import ml_dtypes
import numpy as np
from jax import lax
from jax.experimental import pallas as pl
from jax.experimental.pallas import tpu as pltpu
from jax.sharding import PartitionSpec as P

theta_cheb = 1.125
delta_cheb = 0.875
start_points = [
    -0.8717401485096066,
    -0.5917001814331423,
    -0.2092992179024789,
    0.2092992179024789,
    0.5917001814331423,
    0.8717401485096066,
]


def legendre_pair(value):
    before, now = (1.0, value)
    for order in range(1, 7):
        before, now = (now, ((2 * order + 1) * value * now - order * before) / (order + 1))
    return (now, before)


def lobatto_tables():
    point_list = [-1.0]
    for guess in start_points:
        place = guess
        for newton in range(4):
            seventh, sixth = legendre_pair(place)
            slope = 7.0 * (place * seventh - sixth) / (place * place - 1.0)
            curve = (2.0 * place * slope - 56.0 * seventh) / (1.0 - place * place)
            place = place - slope / curve
        point_list.append(place)
    point_list.append(1.0)
    sample_nodes_list = np.array(point_list)
    values = np.array([legendre_pair(place)[0] for place in point_list])
    weights = 2.0 / (56.0 * values * values)
    derivative = np.zeros((8, 8))
    for i in range(8):
        for j in range(8):
            if i != j:
                derivative[i, j] = values[i] / (
                    values[j] * (sample_nodes_list[i] - sample_nodes_list[j])
                )
    derivative[0, 0] = -14.0
    derivative[7, 7] = 14.0
    stiffness = derivative.T @ (weights[:, None] * derivative)
    return (sample_nodes_list, weights, stiffness)


def assemble(elements, stiffness, weights):
    width = 7 * elements + 1
    assembled = np.zeros((width, width))
    masses = np.zeros(width)
    for e in range(elements):
        assembled[7 * e : 7 * e + 8, 7 * e : 7 * e + 8] += stiffness
        masses[7 * e : 7 * e + 8] += weights
    return (assembled, masses)


def jacobi_eigen(matrix):
    order = matrix.shape[0]
    work = [[float(matrix[i, j]) for j in range(order)] for i in range(order)]
    vectors = [[1.0 if i == j else 0.0 for j in range(order)] for i in range(order)]
    for sweep in range(12):
        for p in range(order):
            for q in range(p + 1, order):
                angle = 0.5 * math.atan2(2.0 * work[p][q], work[q][q] - work[p][p])
                cosine = math.cos(angle)
                sine = math.sin(angle)
                for k in range(order):
                    left, right = (work[k][p], work[k][q])
                    work[k][p] = cosine * left - sine * right
                    work[k][q] = sine * left + cosine * right
                for k in range(order):
                    left, right = (work[p][k], work[q][k])
                    work[p][k] = cosine * left - sine * right
                    work[q][k] = sine * left + cosine * right
                for k in range(order):
                    left, right = (vectors[k][p], vectors[k][q])
                    vectors[k][p] = cosine * left - sine * right
                    vectors[k][q] = sine * left + cosine * right
    return (np.array([work[i][i] for i in range(order)]), np.array(vectors))


def schwarz_basis():
    sample_nodes_list, weights, stiffness = lobatto_tables()
    assembled, masses = assemble(3, stiffness, weights)
    block_stiff = assembled[6:16, 6:16]
    inv_root = 1.0 / np.sqrt(masses[6:16])
    eigen_vals, eigen_vecs = jacobi_eigen(inv_root[:, None] * block_stiff * inv_root[None, :])
    return (inv_root[:, None] * eigen_vecs, eigen_vals)


def forward_table(elements, eigen_basis):
    matrix = np.zeros((10 * elements, 7 * elements + 4))
    for j in range(elements):
        matrix[10 * j : 10 * j + 10, 7 * j + 1 : 7 * j + 11] = eigen_basis.T
    return matrix


def backward_table(elements, eigen_basis):
    matrix = np.zeros((7 * elements, 10 * elements))
    for j in range(elements):
        matrix[7 * j : 7 * j + 7, 10 * j : 10 * j + 10] = eigen_basis[1:8]
    return matrix


def injection_coefficients(elements, sample_nodes_list):
    matrix = np.zeros((elements + 1, 7 * elements))
    for e in range(elements):
        for m in range(7):
            matrix[e, 7 * e + m] += (1.0 - sample_nodes_list[m]) / 2.0
            matrix[e + 1, 7 * e + m] += (1.0 + sample_nodes_list[m]) / 2.0
    return matrix


def sine_modes(vertex, elements):
    modes = np.arange(elements)
    angles = np.pi * modes / elements
    entries = np.sqrt(2.0 / elements) * np.sin(
        np.pi * (np.asarray(vertex)[:, None] * modes[None, :] % (2 * elements)) / elements
    )
    entries = entries / np.sqrt((4.0 + 2.0 * np.cos(angles)) / 3.0)[None, :]
    return np.where(modes[None, :] > 0, entries, 0.0)


def coarse_eigen(elements):
    angles = np.pi * np.arange(elements) / elements
    return np.where(
        np.arange(elements) > 0, 3.0 * (1.0 - np.cos(angles)) / (4.0 + 2.0 * np.cos(angles)), 1.0
    )


class Pack:
    def __init__(self, width):
        self.width, self.rows, self.blocks = (width, 0, [])

    def put(self, row, lane, matrix):
        self.blocks.append((row, lane, np.asarray(matrix)))
        self.rows = max(self.rows, row + -(-matrix.shape[0] // 16) * 16)
        return (slice(row, row + matrix.shape[0]), slice(lane, lane + matrix.shape[1]))

    def add(self, matrix, count=2):
        parts = []
        for _ in range(count):
            parts.append(np.asarray(matrix).astype(ml_dtypes.bfloat16))
            matrix = matrix - parts[-1].astype(np.float64)
        row, step = (self.rows, max(128, -(-matrix.shape[1] // 128) * 128))
        places = []
        for number, part in enumerate(parts):
            if step * count <= self.width:
                places.append(self.put(row, step * number, part))
            else:
                places.append(self.put(self.rows, 0, part))
        return tuple(places)

    def array(self, dtype, rows=0):
        whole = np.zeros((max(self.rows, rows), self.width), dtype)
        for row, lane, matrix in self.blocks:
            whole[row : row + matrix.shape[0], lane : lane + matrix.shape[1]] = matrix
        return whole


def parts(ref, places):
    return tuple(ref[place] for place in places)


def whole(ref, places, rows=None):
    if rows is not None:
        places = [(rows, lanes) for _, lanes in places]
    high, middle, low = (ref[place].astype(jnp.float32) for place in places)
    return high + (middle + low)


def split(value):
    high = value.astype(jnp.bfloat16)
    return (high, (value - high.astype(jnp.float32)).astype(jnp.bfloat16))


def dot3(left, right):
    def mul(a, b):
        return jnp.dot(a, b, preferred_element_type=jnp.float32)

    return mul(left[0], right[0]) + (mul(left[0], right[1]) + mul(left[1], right[0]))


def dot32(left, right):
    return jnp.dot(
        left, right, precision=lax.Precision.HIGHEST, preferred_element_type=jnp.float32
    )


NONE = None
OWN = list(range(14)) + [NONE, NONE]
X_RING = OWN[:14] + [14, 15, -1]
Y_RING = OWN + [14, 15, -1] + [NONE] * 5
EDGE = [0, 1, NONE, 13] + [NONE] * 4
VERTICES = [(0, 0), (0, 1), (1, 0), (1, 1), (0, 2), (1, 2), (2, 0), (2, 1), (2, 2)]
LOADER_ROOM = 48
EARLY_ROWS = 20 * 1024


def pick(matrix, rows, columns, row_zero, column_zero):
    result = np.zeros((len(rows), len(columns)))
    for i, row in enumerate(rows):
        for j, column in enumerate(columns):
            if row is not None and column is not None:
                result[i, j] = matrix[row + row_zero, column + column_zero]
    return result


def pick_vector(vector, slots, zero):
    return np.array([0.0 if slot is None else vector[slot + zero] for slot in slots])


class Tables:
    def __init__(self, elements_z, count_x, count_y):
        points, weights, stiffness = lobatto_tables()
        basis, values = schwarz_basis()
        nodes_z = 7 * elements_z
        half = elements_z // 2
        self.cut = cut = (7 * half) // 128 * 128
        self.first = first = min(256, nodes_z)
        self.stiffness = stiffness
        smoother, second = (Pack(512), Pack(512))
        mask_z = np.arange(nodes_z) > 0

        ahead = forward_table(2, basis)
        back = backward_table(2, basis)
        back_y = np.zeros((16, 20))
        back_y[:14] = back
        ahead_x = pick(ahead, range(20), X_RING, 0, 2)
        self.ahead_own = smoother.add(np.kron(ahead_x, pick(ahead, range(20), OWN, 0, 2)))
        ahead_edge = pick(ahead, range(20), Y_RING[16:], 0, 2)
        ahead_edge[:, 3] = -ahead[:, 2]
        ahead_edge[:, 4] = -(ahead[:, 9:16] @ stiffness[:7, 7])
        self.ahead_edge = smoother.add(np.kron(ahead_x, ahead_edge))
        self.back_xy = smoother.add(np.kron(back, back_y))
        all_ahead = forward_table(elements_z, basis)[:, 2 : 2 + nodes_z].T * mask_z[:, None]
        all_back = backward_table(elements_z, basis).T * mask_z[None, :]
        self.ahead_z, self.back_z, self.value_columns = ([], [], [])
        for low, high, base, stop in ((0, half, 0, first), (half, elements_z, cut, nodes_z)):
            modes, width = (slice(10 * low, 10 * high), 10 * (high - low))
            assert not all_ahead[:base, modes].any() and not all_ahead[stop:, modes].any()
            assert not all_back[modes, :base].any() and not all_back[modes, stop:].any()
            ahead_z, back_z = (np.zeros((stop - base, 256)), np.zeros((256, stop - base)))
            ahead_z[:, :width] = all_ahead[base:stop, modes]
            back_z[:width] = all_back[modes, base:stop]
            columns = np.ones((1, 256))
            columns[0, :width] = np.tile(values, high - low)
            self.ahead_z.append(smoother.add(ahead_z))
            self.back_z.append(smoother.add(back_z))
            self.value_columns.append(smoother.add(columns, 3))
        rows = np.add.outer(np.tile(values, 2), np.tile(values, 2)).reshape(400, 1)
        self.value_rows = smoother.add(rows, 3)

        pair, _ = assemble(2, stiffness, weights)
        _, mass = assemble(4, stiffness, weights)
        stiff_x = np.zeros((17, 21))
        stiff_x[:15, :15] = pair
        stiff_x[0, 0] += stiffness[7, 7]
        stiff_x[16, 0] = stiffness[6, 7]
        for row, column in ((0, 17), (16, 18), (14, 19), (15, 20)):
            stiff_x[row, column] = 1.0
        stiff_y = np.zeros((16, 16))
        stiff_y[:14, :14] = pair[:14, :14]
        stiff_y[0, 0] += stiffness[7, 7]
        edge_y = np.zeros((8, 16))
        edge_y[0, 0:8], edge_y[1, 0:8], edge_y[2, 0] = (stiffness[0], stiffness[1], 1.0)
        edge_y[3, 7:14], edge_y[4, 7:14] = (stiffness[6, :7], stiffness[7, :7])
        mass_x, mass_y = (pick_vector(mass, X_RING, 7), pick_vector(mass, OWN, 7))
        mass_edge = pick_vector(mass, EDGE, 7)
        batches = ((0, 8), (8, 16), (16, 17))
        self.batches = batches
        self.edge_x = second.add(np.kron(stiff_x, np.diag(mass_edge)))
        self.edge_y = [
            second.add(np.kron(np.diag(mass_x[low:high]), edge_y)) for low, high in batches
        ]
        self.own_x = [
            second.add(np.kron(stiff_x, np.diag(mass_y[low : low + 8]))) for low in (0, 8)
        ]
        self.own_y = [
            second.add(np.kron(np.diag(mass_x[low:high]), stiff_y)) for low, high in batches
        ]
        self.mass_edge = second.add(np.outer(mass_x, mass_edge).reshape(-1, 1), 3)
        self.mass_own = second.add(np.outer(mass_x, mass_y).reshape(-1, 1), 3)
        stiff_z, line_z = assemble(elements_z, stiffness, weights)
        stiff_z, line_z = (stiff_z[:nodes_z, :nodes_z], line_z[:nodes_z])
        self.mass_z = second.add(line_z[None, :], 3)
        low_z, high_z = (stiff_z[:first, :first].copy(), stiff_z[cut:, cut:].copy())
        low_z[:, 7 * half :] = 0.0
        high_z[:, : 7 * half - cut] = 0.0
        self.stiff_z = [second.add(low_z), second.add(high_z)]

        stiff3, mass3 = assemble(3, stiffness, weights)
        inject = np.zeros((4, 22))
        inject[:, :21] = injection_coefficients(3, points)
        inject[3, 21] = 1.0

        def padded(matrix):
            wide = np.zeros((matrix.shape[0], 16))
            wide[:, :14] = matrix
            return wide

        drop = inject[:, 7:21]
        drop_mass = (inject * mass3[None, :])[:, 7:21]
        drop_stiff = (inject @ stiff3)[:, 7:21]
        self.drop_b = second.add(np.kron(drop, padded(drop)))
        across = np.kron(drop_stiff, padded(drop_mass)) + np.kron(drop_mass, padded(drop_stiff))
        self.drop_x = second.add(
            -np.concatenate([across, np.kron(drop_mass, padded(drop_mass))])
        )
        drop_z = injection_coefficients(elements_z, points)[:elements_z]
        phi_z = sine_modes(np.arange(elements_z), elements_z)
        masked_z = (drop_z * mask_z[None, :]).T
        modes_z = np.zeros((nodes_z, 384))
        for part, matrix in enumerate((masked_z, line_z[:, None] * masked_z, stiff_z @ masked_z)):
            for base in (128 * part, 128 * part + 64):
                modes_z[:, base : base + elements_z] = matrix @ phi_z
        self.modes_z = second.add(modes_z)

        sides_x, sides_y = (count_x // 2, count_y // 2)
        phi_x = sine_modes(np.arange(count_x + 1), count_x)
        phi_y = sine_modes(np.arange(count_y + 1), count_y)
        lam_x, lam_y = (coarse_eigen(count_x), coarse_eigen(count_y))
        assert elements_z <= 64
        eigen_z = coarse_eigen(elements_z)
        eye_x = np.eye(4)
        to_y = np.zeros((sides_y, sides_y, 4, 2, 4, 4))
        from_y = np.zeros((sides_y, 2, 16, sides_y, 4))
        eigen_yz = np.ones((sides_y, 2, 64))
        for place in range(sides_y):
            eigen_yz[place, :, :elements_z] = (
                lam_y[2 * place : 2 * place + 2, None] + eigen_z[None, :]
            )
            for j in range(4):
                if 2 * place + j - 1 >= 0:
                    row = phi_y[2 * place + j - 1].reshape(sides_y, 2)
                    to_y[place, :, :, :, :, j] = (
                        eye_x[None, :, None, :] * row[:, None, :, None]
                    )
            for number, (i, j) in enumerate(VERTICES):
                row = phi_y[2 * place + j].reshape(sides_y, 2)
                from_y[place, :, number, :, i] = row.T
        to_x = np.zeros((count_x, sides_x, 4))
        from_x = np.zeros((sides_x, 16, count_x))
        for place in range(sides_x):
            for i in range(4):
                if 2 * place + i - 1 >= 0:
                    to_x[:, place, i] = phi_x[2 * place + i - 1]
            from_x[place, :3] = phi_x[2 * place : 2 * place + 3]
        self.sent = sent = 4 * sides_y
        self.count_x = count_x
        height = -(-sent // 16) * 16
        places = Pack(512)
        for place in range(sides_y):
            rows = np.zeros((height + 48, 128))
            rows[:sent, :32] = to_y[place].reshape(sent, 32)
            rows[height : height + 32, :sent] = from_y[place].reshape(32, sent)
            rows[height + 32] = eigen_yz[place].ravel()
            places.add(rows, 3)
        self.height = height
        self.place_x_base = places.rows
        for place in range(sides_x):
            rows = np.zeros((16, 128))
            rows[:, :count_x] = from_x[place]
            places.add(rows, 3)
        lift = injection_coefficients(2, points)
        lift_xy = np.zeros((14, 16, 16))
        for number, (i, j) in enumerate(VERTICES):
            lift_xy[:, :14, number] = np.outer(lift[i], lift[j])
        lift_z, back_phi = (np.zeros((128, nodes_z)), np.zeros((128, elements_z)))
        for base in (0, 64):
            lift_z[base : base + elements_z] = phi_z.T @ drop_z * mask_z[None, :]
            back_phi[base : base + elements_z] = phi_z.T
        late = Pack(512)
        self.to_modes_x = late.put(0, 0, to_x.reshape(count_x, 4 * sides_x))
        self.lift_xy = late.put(0, 256, lift_xy.reshape(224, 16))
        self.eigen_x = late.put(0, 384, lam_x[:, None])
        self.lift_z = late.put(224, 0, lift_z)
        self.phi_z = late.put(224, 384, back_phi)

        self.late = late.array(np.float32)
        self.smoother_rows, self.second_rows = (smoother.rows, second.rows)
        self.places_base = smoother.rows + second.rows
        self.early = np.zeros((EARLY_ROWS, 512), ml_dtypes.bfloat16)
        stacked = [pack.array(ml_dtypes.bfloat16) for pack in (smoother, second, places)]
        used = np.concatenate(stacked)
        self.early[: used.shape[0]] = used
        self.place_parts = tuple(
            (slice(None), slice(128 * part, 128 * part + 128)) for part in range(3)
        )


def sides_of(places, sides):
    flags = []
    for axis in range(2):
        flags.append(jnp.where(places[axis] > 0, 1.0, 0.0))
        flags.append(jnp.where(places[axis] < sides[axis] - 1, 1.0, 0.0))
    return flags


def line_mask(flags):
    x = lax.broadcasted_iota(jnp.int32, (17, 16, 1), 0)
    y = lax.broadcasted_iota(jnp.int32, (17, 16, 1), 1)
    keep_x = jnp.where((x == 0) | (x == 16), flags[0], jnp.where(x >= 14, flags[1], 1.0))
    return keep_x * jnp.where(y == 0, flags[2], 1.0)


def edge_mask(flags):
    x = lax.broadcasted_iota(jnp.int32, (17, 8, 1), 0)
    slot = lax.broadcasted_iota(jnp.int32, (17, 8, 1), 1)
    keep_x = jnp.where((x == 0) | (x == 16), flags[0], jnp.where(x >= 14, flags[1], 1.0))
    return keep_x * jnp.where((slot == 2) | (slot == 3), flags[2], flags[3])


def own_mask(flags):
    x = lax.broadcasted_iota(jnp.int32, (14, 16, 1), 0)
    y = lax.broadcasted_iota(jnp.int32, (14, 16, 1), 1)
    return jnp.where(x == 0, flags[0], 1.0) * jnp.where(y == 0, flags[2], 1.0)


def join_z(low, high, cut):
    middle = low.shape[1]
    return jnp.concatenate(
        [low[:, :cut], low[:, cut:] + high[:, : middle - cut], high[:, middle - cut :]], axis=1
    )


def schwarz(modes, edge, tables, smoother):
    cut = tables.cut
    edge = split(edge.reshape(136, edge.shape[2]))
    modes = modes + dot3(parts(smoother, tables.ahead_edge), edge)
    rows = whole(smoother, tables.value_rows)
    halves = []
    for number, block in enumerate((modes[:, : tables.first], modes[:, cut:])):
        block = dot3(split(block), parts(smoother, tables.ahead_z[number]))
        block = block / (rows + whole(smoother, tables.value_columns[number]))
        halves.append(dot3(split(block), parts(smoother, tables.back_z[number])))
    return dot3(parts(smoother, tables.back_xy), split(join_z(*halves, cut)))


class Shape(tuple):
    dtype = jnp.float32


class HalfShape(Shape):
    dtype = jnp.bfloat16


def kernel_call(body, inputs, outputs, scratch=(), spaces={}, flops=0, moved=0, room=4):
    def kernel(*refs):
        last = len(inputs) + len(outputs)
        body(refs[: len(inputs)], refs[len(inputs) : last], refs[last:])

    return pl.pallas_call(
        kernel,
        out_shape=[jax.ShapeDtypeStruct(shape, shape.dtype) for shape in outputs],
        in_specs=[
            pl.BlockSpec(memory_space=spaces.get(number, pltpu.VMEM))
            for number in range(len(inputs))
        ],
        out_specs=[pl.BlockSpec(memory_space=pltpu.VMEM) for _ in outputs],
        scratch_shapes=list(scratch),
        compiler_params=pltpu.CompilerParams(vmem_limit_bytes=room * 1024 * 1024),
        cost_estimate=pl.CostEstimate(flops=flops, bytes_accessed=moved, transcendentals=0),
    )(*inputs)


def run_copies(pairs, semaphores):
    copies = [
        pltpu.make_async_copy(source, target, semaphores.at[number])
        for number, (source, target) in enumerate(pairs)
    ]
    for copy in copies:
        copy.start()
    for copy in copies:
        copy.wait()


def load_smoother(tables):
    def body(ins, outs, scratch):
        run_copies([(ins[0].at[0 : tables.smoother_rows], outs[0])], scratch[0])

    return body


def load_second(tables):
    def body(ins, outs, scratch):
        early, places, _ = ins
        base = tables.smoother_rows
        size = tables.height + 48
        row_y = pl.multiple_of(tables.places_base + size * places[1], 16)
        row_x = pl.multiple_of(tables.places_base + tables.place_x_base + 16 * places[0], 16)
        run_copies(
            [
                (early.at[base : base + tables.second_rows], outs[0]),
                (early.at[pl.ds(row_y, size)], outs[1]),
                (early.at[pl.ds(row_x, 16)], outs[2]),
            ],
            scratch[0],
        )

    return body


def first_x_rows(ins, outs, scratch):
    outs[0][...] = ins[0][...]
    outs[1][...] = ins[0][0:2]
    outs[2][...] = ins[0][13:14]


def first_y_rows(ins, outs, scratch):
    own, x_low, x_high, _ = ins
    for out, rows in zip(outs, (slice(0, 2), slice(13, 14))):
        out[0:14] = own[:, rows]
        out[14:16] = x_high[:, rows]
        out[16:17] = x_low[:, rows]


def own_modes(tables, sides):
    def body(ins, outs, scratch):
        places, own, x_low, x_high, smoother = ins
        (line,) = scratch
        nodes_z = own.shape[2]
        line[:, 14:16] = jnp.zeros((17, 2, nodes_z), jnp.float32)
        line[0:14, 0:14] = own[...]
        line[14:16, 0:14] = x_high[...]
        line[16:17, 0:14] = x_low[...]
        masked = line[...] * line_mask(sides_of(places, sides))
        outs[0][...] = masked
        rows = split(masked.reshape(272, nodes_z))
        outs[1][...] = dot3(parts(smoother, tables.ahead_own), rows)

    return body


def first_sweep(tables, sides):
    def body(ins, outs, scratch):
        places, modes, y_low, y_high, smoother = ins
        flags = sides_of(places, sides)
        nodes_z = modes.shape[1]
        edge = outs[1]
        edge[:, 0:2] = y_high[...]
        edge[:, 2:3] = y_low[...]
        edge[:, 3:8] = jnp.zeros((17, 5, nodes_z), jnp.float32)
        edge[...] = edge[...] * edge_mask(flags)
        result = schwarz(modes[...], edge[...], tables, smoother)
        result = result.reshape(14, 16, nodes_z) * (own_mask(flags) * (1.0 / theta_cheb))
        result = result[:, :14]
        outs[0][...] = result
        stiffness = tables.stiffness
        outs[2][0:2] = result[0:2]
        outs[3][0:1] = result[13:14]
        for row in range(2):
            outs[2][2 + row] = sum(float(stiffness[row, j]) * result[j] for j in range(8))
            outs[3][1 + row] = sum(float(stiffness[7 - row, j]) * result[7 + j] for j in range(7))

    return body


def fill_lines(line, own, x_low, x_high):
    line[:, 14:16] = jnp.zeros((21, 2, own.shape[2]), jnp.float32)
    line[0:14, 0:14] = own[...]
    line[14:16, 0:14] = x_high[0:2]
    line[16:19, 0:14] = x_low[...]
    line[19:21, 0:14] = x_high[2:4]


def apply_z(rows, tables, second):
    return join_z(
        dot3(split(rows[:, : tables.first]), parts(second, tables.stiff_z[0])),
        dot3(split(rows[:, tables.cut :]), parts(second, tables.stiff_z[1])),
        tables.cut,
    )


def edge_rows(tables):
    def body(ins, outs, scratch):
        own, x_low, x_high, second = ins
        line, edge, total = scratch
        nodes_z = own.shape[2]
        fill_lines(line, own, x_low, x_high)
        edge[...] = jnp.zeros((21, 8, nodes_z), jnp.float32)
        edge[:, 0:2] = line[:, 0:2]
        edge[:, 3:4] = line[:, 13:14]
        part = dot3(parts(second, tables.edge_x), split(edge[...].reshape(168, nodes_z)))
        total[...] = part.reshape(17, 8, nodes_z)
        for places, (low, high) in zip(tables.edge_y, tables.batches):
            rows = line[low:high].reshape(16 * (high - low), nodes_z)
            part = dot3(parts(second, places), split(rows))
            total[low:high] += part.reshape(high - low, 8, nodes_z)
        along = apply_z(edge[0:17].reshape(136, nodes_z), tables, second)
        result = total[...].reshape(136, nodes_z) * whole(second, tables.mass_z)
        result = result + whole(second, tables.mass_edge) * along
        total[...] = result.reshape(17, 8, nodes_z)
        outs[0][...] = total[:, 0:3]
        outs[1][...] = total[:, 3:5]

    return body


def own_rows(tables, sides):
    def body(ins, outs, scratch):
        own, x_low, x_high, second, places, source, smoother = ins
        line, total = scratch
        modes, from_b = outs
        nodes_z = own.shape[2]
        fill_lines(line, own, x_low, x_high)
        for number, place in enumerate(tables.own_x):
            rows = line[:, 8 * number : 8 * number + 8].reshape(168, nodes_z)
            part = dot3(parts(second, place), split(rows))
            total[:, 8 * number : 8 * number + 8] = part.reshape(17, 8, nodes_z)
        for place, (low, high) in zip(tables.own_y, tables.batches):
            rows = line[low:high].reshape(16 * (high - low), nodes_z)
            part = dot3(parts(second, place), split(rows))
            total[low:high] += part.reshape(high - low, 16, nodes_z)
        along = apply_z(line[0:17].reshape(272, nodes_z), tables, second)
        applied = total[...].reshape(272, nodes_z) * whole(second, tables.mass_z)
        applied = applied + whole(second, tables.mass_own) * along
        remain = (source[...] - applied.reshape(17, 16, nodes_z)) * line_mask(sides_of(places, sides))
        modes[...] = dot3(parts(smoother, tables.ahead_own), split(remain.reshape(272, nodes_z)))
        rows = source[0:14].reshape(224, nodes_z)
        from_b[...] = dot3(parts(second, tables.drop_b), split(rows))

    return body


def second_sweep(tables, sides, scale_old, scale_new):
    def body(ins, outs, scratch):
        places, own, modes, to_low, to_high, y_low, y_high, source, from_b = ins[:9]
        smoother, second, place_y = ins[9:]
        edge, update = scratch
        flags = sides_of(places, sides)
        nodes_z = own.shape[2]
        stiffness = tables.stiffness
        above = y_high[:, 2:3]
        edge[:, 0:1] = source[:, 0:1] - (
            y_high[:, 0:1] + to_high[:, 1:2] + float(stiffness[7, 7]) * above
        )
        edge[:, 1:2] = source[:, 1:2] - y_high[:, 1:2]
        edge[:, 2:3] = source[:, 2:3] - (y_low[:, 0:1] + float(stiffness[6, 7]) * to_low[:, 2:3])
        edge[:, 3:4] = y_low[:, 1:2]
        edge[:, 4:5] = above
        edge[:, 5:8] = jnp.zeros((17, 3, nodes_z), jnp.float32)
        result = schwarz(modes[...], edge[...] * edge_mask(flags), tables, smoother)
        update[...] = result.reshape(14, 16, nodes_z) * (own_mask(flags) * scale_new)
        update[:, 0:14] += (1.0 + scale_old) * own[...]
        outs[0][...] = update[:, 0:14]
        from_x = dot3(parts(second, tables.drop_x), split(update[...].reshape(224, nodes_z)))
        both = jnp.concatenate([from_b[...], from_x], axis=0)
        modes = dot3(split(both), parts(second, tables.modes_z))
        modes = modes[0:16, 0:128] + modes[16:32, 128:256] + modes[32:48, 256:384]
        left = lax.broadcasted_iota(jnp.int32, (16, 128), 1) < 64
        modes = jnp.concatenate([jnp.where(left, modes, 0.0), jnp.where(left, 0.0, modes)], axis=0)
        to_modes_y = whole(place_y, tables.place_parts, slice(0, tables.sent))[:, 0:32]
        outs[1][...] = dot32(to_modes_y, modes).reshape(outs[1].shape)

    return body


def sum_modes_y(ins, outs, scratch):
    outs[0][...] = jnp.broadcast_to(jnp.sum(ins[0][...], axis=0, keepdims=True), outs[0].shape)


def solve_modes(tables):
    def body(ins, outs, scratch):
        arrived, late, place_x, place_y = ins
        modes = dot32(late[tables.to_modes_x], arrived[...].reshape(-1, 128))
        row = tables.height + 32
        eigen_yz = whole(place_y, tables.place_parts, slice(row, row + 16))[0:1]
        modes = modes / (late[tables.eigen_x] + eigen_yz)
        back = dot32(whole(place_x, tables.place_parts)[0:8, 0 : tables.count_x], modes)
        outs[0][...] = jnp.broadcast_to(back[None, 0:4], outs[0].shape)

    return body


def finish(tables, sides):
    def body(ins, outs, scratch):
        places, arrived, approx, late, place_y = ins
        nodes_z = approx.shape[2]
        rows = slice(tables.height, tables.height + 32)
        from_modes_y = whole(place_y, tables.place_parts, rows)[:, 0 : tables.sent]
        vertices = dot3(split(from_modes_y), split(arrived[...].reshape(-1, 128)))
        left = lax.broadcasted_iota(jnp.int32, (16, 128), 1) < 64
        vertices = split(jnp.where(left, vertices[0:16], vertices[16:32]))
        coarse = dot3(vertices, split(late[tables.phi_z]))
        outs[1][0] = coarse[0:2]
        outs[1][1] = coarse[2:4]
        lines = dot3(vertices, split(late[tables.lift_z]))
        fine = dot3(split(late[tables.lift_xy]), split(lines))
        fine = fine.reshape(14, 16, nodes_z) * own_mask(sides_of(places, sides))
        outs[0][...] = approx[...] + fine[:, :14]

    return body


def shift(block, axis, distance):
    count = lax.axis_size(axis)
    route = [((i - distance) % count, i) for i in range(count)]
    if axis == "gx":
        route = [(i, j) for i, j in route if j - i == distance]
    return lax.ppermute(block, axis, route)


def per_device(residual_in):
    nodes_x, nodes_y, nodes_z = residual_in.shape
    assert nodes_x == 14 and nodes_y == 14 and nodes_z % 14 == 0
    sides = (lax.axis_size("gx"), lax.axis_size("gy"))
    places = jnp.stack([lax.axis_index("gx"), lax.axis_index("gy")]).astype(jnp.int32)
    elements_z = nodes_z // 7
    tables = Tables(elements_z, 2 * sides[0], 2 * sides[1])
    early, late = (jnp.asarray(tables.early), jnp.asarray(tables.late))
    sigma_ratio = theta_cheb / delta_cheb
    rho_now = 1.0 / sigma_ratio
    rho_next = 1.0 / (2.0 * sigma_ratio - rho_now)
    scalars = {0: pltpu.SMEM}

    def block(*shape):
        return Shape(shape + (nodes_z,))

    def scratch(*shape):
        return pltpu.VMEM(shape + (nodes_z,), jnp.float32)

    own, to_low, to_high = kernel_call(
        first_x_rows, [residual_in], [block(14, 14), block(2, 14), block(1, 14)]
    )
    x_low, x_high = (shift(to_high, "gx", 1), shift(to_low, "gx", -1))
    (smoother,) = kernel_call(
        load_smoother(tables),
        [early],
        [HalfShape((tables.smoother_rows, 512))],
        [pltpu.SemaphoreType.DMA((1,))],
        {0: pl.ANY},
        moved=6_000_000,
        room=LOADER_ROOM,
    )
    to_low, to_high = kernel_call(
        first_y_rows, [own, x_low, x_high, smoother], [block(17, 2), block(17, 1)]
    )
    y_low, y_high = (shift(to_high, "gy", 1), shift(to_low, "gy", -1))
    source, modes = kernel_call(
        own_modes(tables, sides),
        [places, own, x_low, x_high, smoother],
        [block(17, 16), block(400)],
        [scratch(17, 16)],
        scalars,
        flops=500_000_000,
        moved=2_000_000,
        room=8,
    )
    direction, edge, to_low, to_high = kernel_call(
        first_sweep(tables, sides),
        [places, modes, y_low, y_high, smoother],
        [block(14, 14), block(17, 8), block(4, 14), block(3, 14)],
        (),
        scalars,
        flops=2_000_000_000,
        moved=4_000_000,
        room=8,
    )
    x_low, x_high = (shift(to_high, "gx", 1), shift(to_low, "gx", -1))
    second, place_y, place_x = kernel_call(
        load_second(tables),
        [early, places, to_low],
        [
            HalfShape((tables.second_rows, 512)),
            HalfShape((tables.height + 48, 512)),
            HalfShape((16, 512)),
        ],
        [pltpu.SemaphoreType.DMA((3,))],
        {0: pl.ANY, 1: pltpu.SMEM},
        moved=6_000_000,
        room=LOADER_ROOM,
    )
    lines = [direction, x_low, x_high, second]
    to_low, to_high = kernel_call(
        edge_rows(tables),
        lines,
        [block(17, 3), block(17, 2)],
        [scratch(21, 16), scratch(21, 8), scratch(17, 8)],
        flops=500_000_000,
        moved=2_000_000,
        room=8,
    )
    y_low, y_high = (shift(to_high, "gy", 1), shift(to_low, "gy", -1))
    modes, from_b = kernel_call(
        own_rows(tables, sides),
        lines + [places, source, smoother],
        [block(400), block(16)],
        [scratch(21, 16), scratch(17, 16)],
        {4: pltpu.SMEM},
        flops=1_500_000_000,
        moved=3_000_000,
        room=8,
    )
    approx, outgoing = kernel_call(
        second_sweep(tables, sides, rho_next * rho_now, 2.0 * rho_next / delta_cheb),
        [places, direction, modes, to_low, to_high, y_low, y_high, edge, from_b]
        + [smoother, second, place_y],
        [block(14, 14), Shape((sides[1], 4, 128))],
        [scratch(17, 8), scratch(14, 16)],
        scalars,
        flops=3_000_000_000,
        moved=6_000_000,
        room=8,
    )
    arrived = lax.all_to_all(outgoing, "gy", 0, 0, tiled=True)
    (outgoing,) = kernel_call(sum_modes_y, [arrived], [Shape((sides[0], 4, 128))])
    arrived = lax.all_to_all(outgoing, "gx", 0, 0, tiled=True)
    (outgoing,) = kernel_call(
        solve_modes(tables), [arrived, late, place_x, place_y], [Shape((sides[1], 4, 128))]
    )
    arrived = lax.all_to_all(outgoing, "gy", 0, 0, tiled=True)
    correction, coarse = kernel_call(
        finish(tables, sides),
        [places, arrived, approx, late, place_y],
        [block(14, 14), Shape((2, 2, elements_z))],
        (),
        scalars,
    )
    return (correction, coarse)


def solution(mesh):
    return jax.shard_map(
        per_device,
        mesh=mesh,
        in_specs=(P("gx", "gy", None),),
        out_specs=(P("gx", "gy", None), P("gx", "gy", None)),
        check_vma=False,
    )
```

time: 684 us -> 95.8 us (0.14); the launches traced: 674 us -> 95.4 us
  waiting for transfers between devices: 312 us -> 2.35 us
  local copies, waits for them, and re-layouts: 157 us -> 0.99 us
  matrix products: 45 us -> 0 us
  starting transfers between devices: 56.3 us -> 19.9 us
  blocking collectives: 73.2 us -> 54.6 us
  Pallas kernels: 0 us -> 16.7 us
  between operations: 15.6 us -> 0.78 us
  other arithmetic: 14.8 us -> 0.08 us
    unnamed x2 -> x0, waiting for transfers between devices: 291 us -> none
    scatter-add x6 -> x0, local copies, waits for them, and re-layouts: 81.6 us -> none  [the longest x4 81.3 us: stiff_last(): result = result.at[:, :, 1:, 0].add(operator_output[:, :, :-1, 7])]
    all_gather x1 -> x0, blocking collectives: 73.2 us -> none  [per_device(): gathered_piece = lax.all_gather(scaled, ('gx', 'gy'), axis=0, tiled=True)]
    all_to_all x0 -> x3, blocking collectives: none -> 54.6 us  [the longest x2 28.3 us: per_device(): arrived = lax.all_to_all(outgoing, 'gy', 0, 0, tiled=True)]
    dot_general x29 -> x0, matrix products: 45 us -> none  [the longest x2 7.98 us: smooth(): jnp.einsum('abem,mc->abec', window, basis_small, precision=spectral_radiu...]
    ppermute x18 -> x8, starting transfers between devices: 56.3 us -> 19.9 us  [shift(): return lax.ppermute(block, axis, route)]
    slice x24 -> x0, local copies, waits for them, and re-layouts: 32.9 us -> none  [the longest x6 16.8 us: smooth(): padded[:, :, 7:nodes_z + 7]]
    reshape x13 -> x0, local copies, waits for them, and re-layouts: 31.3 us -> none  [the longest x4 11.1 us: smooth(): padded[:, :, :nodes_z]]
  transfers between devices with their start and end apart: 19 -> 8, of which waited for: 12 -> 2; matrix products, arithmetic and copies ran while one was open for 1% -> 0% of each run, Pallas kernels for 0% -> 8%
where the time goes in v1:
time: 95.8 us; the launch traced here: 95.4 us
  blocking collectives  54.6 us (57%)
  starting transfers between devices  19.9 us (21%)
  Pallas kernels  16.7 us (17%)
  waiting for transfers between devices  2.35 us (2%)
  local copies, waits for them, and re-layouts  0.99 us (1%)
    all_to_all x2, blocking collectives, per_device(): arrived = lax.all_to_all(outgoing, 'gy', 0, 0, tiled=True)  28.3 us
    all_to_all x1, blocking collectives, per_device(): arrived = lax.all_to_all(outgoing, 'gx', 0, 0, tiled=True)  26.3 us
    ppermute x8, starting transfers between devices, shift(): return lax.ppermute(block, axis, route)  19.9 us
    pallas_call x12, Pallas kernels, kernel_call(): pl.pallas_call(kernel, out_shape=[jax.ShapeDtypeStruct(shape, shape.dtype...  16.7 us
    ppermute x8, waiting for transfers between devices, shift(): return lax.ppermute(block, axis, route)  2.35 us
  transfers between devices with their start and end apart: 8, of which 2 were waited for; matrix products, arithmetic and copies ran while one was open for 0% of the time, Pallas kernels for 8%

profile of v1, /device:TPU:1, one launch (start us, length us, event | category | flops | bytes accessed | tf_op | source)
XLA Modules:
  0.0 95.4 jit_solution(518294033483758098)
XLA Ops:
  0.6 0.0 copy-start.1
  0.6 1.0 %copy-done.1 = f32[14,14,336]{2,1,0:T(8,128)S(1)} copy-done((f32[14,14,336]{2,1,0:T(8,128)S(1)}, f32[14,14,336]{2,1,0:T(8,128)}, u32[]{:S(2)}) %copy-start.1) | copy-done | bytes 263448
  1.6 3.9 %collective-permute-start = (f32[1,14,336]{2,1,0:T(8,128)S(1)}, f32[1,14,336]{2,1,0:T(8,128)S(1)}, u32[]{:S(2)}, u32[]{:S(2)}) collective-permute-start(f32[1,14,336]{2,1,0:T(8,128)S(1)} %get-tuple-element.23), channel_id=1, source_target_pairs={{0,16},{16,32},{32,48},{48,64},{64,80},{80,96},{96,112},{112,128},... | collective-permute-start | bytes 56456 | tf_op jit(solution)/shard_map/ppermute | solution.py:712
  5.6 1.3 %collective-permute-start.1 = (f32[2,14,336]{2,1,0:T(8,128)S(1)}, f32[2,14,336]{2,1,0:T(8,128)S(1)}, u32[]{:S(2)}, u32[]{:S(2)}) collective-permute-start(f32[2,14,336]{2,1,0:T(8,128)S(1)} %get-tuple-element.24), channel_id=1, source_target_pairs={{16,0},{32,16},{48,32},{64,48},{80,64},{96,80},{112,96},{128,112},... | collective-permute-start | bytes 112904 | tf_op jit(solution)/shard_map/ppermute | solution.py:712
  6.9 0.1 pad_add_fusion.refs_0_.refs_1_.refs_4_
  7.0 1.9 %shard_map.51.refs_4_.refs_3_.refs_6_.refs_9_ = bf16[3120,512]{1,0:T(8,128)(2,1)S(1)} custom-call(bf16[20480,512]{1,0:T(8,128)(2,1)} %constant.13.clone.refs_0_), custom_call_target="tpu_custom_call" | custom-call | bytes 6000000 | tf_op jit(solution)/shard_map/pallas_call | solution.py:464
  8.9 0.0 collective-permute-done.refs_2_.refs_1_
  8.9 1.5 %collective-permute-done.1.refs_3_.refs_2_ = f32[2,14,336]{2,1,0:T(8,128)S(1)} collective-permute-done((f32[2,14,336]{2,1,0:T(8,128)S(1)}, f32[2,14,336]{2,1,0:T(8,128)S(1)}, u32[]{:S(2)}, u32[]{:S(2)}) %collective-permute-start.1) | collective-permute-done | bytes 37664 | tf_op jit(solution)/shard_map/ppermute | solution.py:712
  10.5 4.1 %collective-permute-start.2 = (f32[17,1,336]{2,1,0:T(1,128)S(1)}, f32[17,1,336]{2,1,0:T(1,128)S(1)}, u32[]{:S(2)}, u32[]{:S(2)}) collective-permute-start(f32[17,1,336]{2,1,0:T(1,128)S(1)} %get-tuple-element.26), channel_id=1, source_target_pairs={{15,0},{0,1},{1,2},{2,3},{3,4},{4,5},{5,6},{6,7},{7,8},{8,9},{9,10... | collective-permute-start | bytes 68552 | tf_op jit(solution)/shard_map/ppermute | solution.py:712
  14.6 1.3 %collective-permute-start.3 = (f32[17,2,336]{2,1,0:T(2,128)S(1)}, f32[17,2,336]{2,1,0:T(2,128)S(1)}, u32[]{:S(2)}, u32[]{:S(2)}) collective-permute-start(f32[17,2,336]{2,1,0:T(2,128)S(1)} %get-tuple-element.27), channel_id=1, source_target_pairs={{1,0},{2,1},{3,2},{4,3},{5,4},{6,5},{7,6},{8,7},{9,8},{10,9},{11,1... | collective-permute-start | bytes 137096 | tf_op jit(solution)/shard_map/ppermute | solution.py:712
  15.9 1.4 %shard_map.52 = (f32[17,16,336]{2,1,0:T(8,128)S(1)}, f32[400,336]{1,0:T(8,128)S(1)}) custom-call(s32[2]{0:T(128)S(1)} %pad_add_fusion.refs_0_.refs_1_.refs_4_, f32[14,14,336]{2,1,0:T(8,128)S(1)} %get-tuple-element.22.refs_1_.refs_0_, f32[1,14,336]{2,1,0:T(8,128)S(1)} %collective-permute-done.refs_2_.refs_1_, ...), custom_call_target="tpu_custom_call" | custom-call | flops 500000000 | bytes 2000000 | tf_op jit(solution)/shard_map/pallas_call | solution.py:464
  17.3 0.0 collective-permute-done.2.refs_2_
  17.3 0.8 collective-permute-done.3.refs_3_
  18.1 2.5 %shard_map.54 = (f32[14,14,336]{2,1,0:T(8,128)S(1)}, f32[17,8,336]{2,1,0:T(8,128)S(1)}, f32[4,14,336]{2,1,0:T(8,128)S(1)}, f32[3,14,336]{2,1,0:T(8,128)S(1)}) custom-call(s32[2]{0:T(128)S(1)} %pad_add_fusion.refs_0_.refs_1_.refs_4_, f32[400,336]{1,0:T(8,128)S(1)} %get-tuple-element.25.refs_1_, f32[17,1,336]{2,1,0:T(1,128)S(1)} %collective-permute-done.2.refs_2_, ...), custom_call_target="tpu_custom_call" | custom-call | flops 2000000000 | bytes 4000000 | tf_op jit(solution)/shard_map/pallas_call | solution.py:464
  20.6 1.3 %collective-permute-start.5 = (f32[4,14,336]{2,1,0:T(8,128)S(1)}, f32[4,14,336]{2,1,0:T(8,128)S(1)}, u32[]{:S(2)}, u32[]{:S(2)}) collective-permute-start(f32[4,14,336]{2,1,0:T(8,128)S(1)} %get-tuple-element.30.refs_2_), channel_id=1, source_target_pairs={{16,0},{32,16},{48,32},{64,48},{80,64},{96,80},{112,96},{128,112},... | collective-permute-start | bytes 225800 | tf_op jit(solution)/shard_map/ppermute | solution.py:712
  21.9 4.0 %collective-permute-start.4 = (f32[3,14,336]{2,1,0:T(8,128)S(1)}, f32[3,14,336]{2,1,0:T(8,128)S(1)}, u32[]{:S(2)}, u32[]{:S(2)}) collective-permute-start(f32[3,14,336]{2,1,0:T(8,128)S(1)} %get-tuple-element.29), channel_id=1, source_target_pairs={{0,16},{16,32},{32,48},{48,64},{64,80},{80,96},{96,112},{112,128},... | collective-permute-start | bytes 169352 | tf_op jit(solution)/shard_map/ppermute | solution.py:712
  25.9 2.3 %shard_map.55 = (bf16[2496,512]{1,0:T(8,128)(2,1)S(1)}, bf16[112,512]{1,0:T(8,128)(2,1)S(1)}, bf16[16,512]{1,0:T(8,128)(2,1)S(1)}) custom-call(bf16[20480,512]{1,0:T(8,128)(2,1)} %constant.13.clone.refs_0_, s32[2]{0:T(128)S(1)} %pad_add_fusion.refs_0_.refs_1_.refs_4_, f32[4,14,336]{2,1,0:T(8,128)S(1)} %get-tuple-element.30.refs_2_), custom_call_target="tpu_custom_call" | custom-call | bytes 6000000 | tf_op jit(solution)/shard_map/pallas_call | solution.py:464
  28.2 0.0 collective-permute-done.4.refs_1_
  28.2 0.0 collective-permute-done.5.refs_2_
  28.3 0.7 shard_map.57
  29.0 0.6 collective-permute-start.6
  29.5 3.4 %collective-permute-start.7 = (f32[17,3,336]{2,1,0:T(4,128)S(1)}, f32[17,3,336]{2,1,0:T(4,128)S(1)}, u32[]{:S(2)}, u32[]{:S(2)}) collective-permute-start(f32[17,3,336]{2,1,0:T(4,128)S(1)} %get-tuple-element.34.refs_3_), channel_id=1, source_target_pairs={{1,0},{2,1},{3,2},{4,3},{5,4},{6,5},{7,6},{8,7},{9,8},{10,9},{11,1... | collective-permute-start | bytes 205640 | tf_op jit(solution)/shard_map/ppermute | solution.py:712
  32.9 2.3 %shard_map.56 = (f32[400,336]{1,0:T(8,128)S(1)}, f32[16,336]{1,0:T(8,128)S(1)}) custom-call(f32[14,14,336]{2,1,0:T(8,128)S(1)} %get-tuple-element.28.refs_0_.refs_1_, f32[3,14,336]{2,1,0:T(8,128)S(1)} %collective-permute-done.4.refs_1_, f32[4,14,336]{2,1,0:T(8,128)S(1)} %collective-permute-done.5.refs_2_, ...), custom_call_target="tpu_custom_call" | custom-call | flops 1500000000 | bytes 3000000 | tf_op jit(solution)/shard_map/pallas_call | solution.py:464
  35.2 0.0 collective-permute-done.6.refs_5_
  35.2 0.0 collective-permute-done.7.refs_6_
  35.2 0.0 copy-start
  35.2 3.2 %shard_map.58 = (f32[14,14,336]{2,1,0:T(8,128)S(1)}, f32[16,4,128]{2,1,0:T(4,128)S(1)}) custom-call(s32[2]{0:T(128)S(1)} %pad_add_fusion.refs_0_.refs_1_.refs_4_, f32[14,14,336]{2,1,0:T(8,128)S(1)} %get-tuple-element.28.refs_0_.refs_1_, f32[400,336]{1,0:T(8,128)S(1)} %get-tuple-element.33.refs_2_, f32[17,3,336]{2,1,0:T(4,128)S(1)} %get-tuple-element.34.refs_3_, ...), custom_call_target="tpu_custom_call" | custom-call | flops 3000000000 | bytes 6000000 | tf_op jit(solution)/shard_map/pallas_call | solution.py:464
  38.5 16.6 %all_to_all.15.refs_0_ = f32[16,4,128]{2,1,0:T(4,128)S(1)} all-to-all(f32[16,4,128]{2,1,0:T(4,128)S(1)} %get-tuple-element.39), channel_id=1, replica_groups=mesh['gx'=32,'gy'=16] {'gy'}, dimensions={0} | all-to-all | bytes 65536 | tf_op jit(solution)/shard_map/all_to_all | solution.py:817
  55.1 26.3 %all_to_all.16.refs_0_ = f32[32,4,128]{2,1,0:T(4,128)S(1)} all-to-all(f32[32,4,128]{2,1,0:T(4,128)S(1)} %shard_map.59), channel_id=1, replica_groups=mesh['gx'=32,'gy'=16] {'gx'}, dimensions={0} | all-to-all | bytes 131072 | tf_op jit(solution)/shard_map/all_to_all | solution.py:819
  81.4 0.3 shard_map.60
  81.7 11.7 %all_to_all.17.refs_1_ = f32[16,4,128]{2,1,0:T(4,128)S(1)} all-to-all(f32[16,4,128]{2,1,0:T(4,128)S(1)} %shard_map.60), channel_id=1, replica_groups=mesh['gx'=32,'gy'=16] {'gy'}, dimensions={0} | all-to-all | bytes 65536 | tf_op jit(solution)/shard_map/all_to_all | solution.py:823
  93.5 1.9 %shard_map.61 = (f32[14,14,336]{2,1,0:T(8,128)}, f32[2,2,48]{2,1,0:T(2,128)}) custom-call(s32[2]{0:T(128)S(1)} %pad_add_fusion.refs_0_.refs_1_.refs_4_, f32[16,4,128]{2,1,0:T(4,128)S(1)} %all_to_all.17.refs_1_, f32[14,14,336]{2,1,0:T(8,128)S(1)} %get-tuple-element.41.refs_2_, f32[352,512]{1,0:T(8,128)S(1)} %copy-done, ...), custom_call_target="tpu_custom_call" | custom-call | tf_op jit(solution)/shard_map/pallas_call | solution.py:464
  (4 shorter events, 0.1 us)
Async XLA Ops:
  0.6 1.0 %copy-start.1 = (f32[14,14,336]{2,1,0:T(8,128)S(1)}, f32[14,14,336]{2,1,0:T(8,128)}, u32[]{:S(2)}) copy-start(f32[14,14,336]{2,1,0:T(8,128)} %refs_0_.3) | copy-start | bytes 790276
  1.6 7.3 %collective-permute-start = (f32[1,14,336]{2,1,0:T(8,128)S(1)}, f32[1,14,336]{2,1,0:T(8,128)S(1)}, u32[]{:S(2)}, u32[]{:S(2)}) collective-permute-start(f32[1,14,336]{2,1,0:T(8,128)S(1)} %get-tuple-element.23), channel_id=1, source_target_pairs={{0,16},{16,32},{32,48},{48,64},{64,80},{80,96},{96,112},{112,128},... | collective-permute-start | bytes 56456 | tf_op jit(solution)/shard_map/ppermute | solution.py:712
  5.6 4.8 %collective-permute-start.1 = (f32[2,14,336]{2,1,0:T(8,128)S(1)}, f32[2,14,336]{2,1,0:T(8,128)S(1)}, u32[]{:S(2)}, u32[]{:S(2)}) collective-permute-start(f32[2,14,336]{2,1,0:T(8,128)S(1)} %get-tuple-element.24), channel_id=1, source_target_pairs={{16,0},{32,16},{48,32},{64,48},{80,64},{96,80},{112,96},{128,112},... | collective-permute-start | bytes 112904 | tf_op jit(solution)/shard_map/ppermute | solution.py:712
  10.5 6.8 %collective-permute-start.2 = (f32[17,1,336]{2,1,0:T(1,128)S(1)}, f32[17,1,336]{2,1,0:T(1,128)S(1)}, u32[]{:S(2)}, u32[]{:S(2)}) collective-permute-start(f32[17,1,336]{2,1,0:T(1,128)S(1)} %get-tuple-element.26), channel_id=1, source_target_pairs={{15,0},{0,1},{1,2},{2,3},{3,4},{4,5},{5,6},{6,7},{7,8},{8,9},{9,10... | collective-permute-start | bytes 68552 | tf_op jit(solution)/shard_map/ppermute | solution.py:712
  14.6 3.5 %collective-permute-start.3 = (f32[17,2,336]{2,1,0:T(2,128)S(1)}, f32[17,2,336]{2,1,0:T(2,128)S(1)}, u32[]{:S(2)}, u32[]{:S(2)}) collective-permute-start(f32[17,2,336]{2,1,0:T(2,128)S(1)} %get-tuple-element.27), channel_id=1, source_target_pairs={{1,0},{2,1},{3,2},{4,3},{5,4},{6,5},{7,6},{8,7},{9,8},{10,9},{11,1... | collective-permute-start | bytes 137096 | tf_op jit(solution)/shard_map/ppermute | solution.py:712
  20.6 7.6 %collective-permute-start.5 = (f32[4,14,336]{2,1,0:T(8,128)S(1)}, f32[4,14,336]{2,1,0:T(8,128)S(1)}, u32[]{:S(2)}, u32[]{:S(2)}) collective-permute-start(f32[4,14,336]{2,1,0:T(8,128)S(1)} %get-tuple-element.30.refs_2_), channel_id=1, source_target_pairs={{16,0},{32,16},{48,32},{64,48},{80,64},{96,80},{112,96},{128,112},... | collective-permute-start | bytes 225800 | tf_op jit(solution)/shard_map/ppermute | solution.py:712
  21.9 6.3 %collective-permute-start.4 = (f32[3,14,336]{2,1,0:T(8,128)S(1)}, f32[3,14,336]{2,1,0:T(8,128)S(1)}, u32[]{:S(2)}, u32[]{:S(2)}) collective-permute-start(f32[3,14,336]{2,1,0:T(8,128)S(1)} %get-tuple-element.29), channel_id=1, source_target_pairs={{0,16},{16,32},{32,48},{48,64},{64,80},{80,96},{96,112},{112,128},... | collective-permute-start | bytes 169352 | tf_op jit(solution)/shard_map/ppermute | solution.py:712
  29.0 6.2 %collective-permute-start.6 = (f32[17,2,336]{2,1,0:T(2,128)S(1)}, f32[17,2,336]{2,1,0:T(2,128)S(1)}, u32[]{:S(2)}, u32[]{:S(2)}) collective-permute-start(f32[17,2,336]{2,1,0:T(2,128)S(1)} %get-tuple-element.35.refs_4_), channel_id=1, source_target_pairs={{15,0},{0,1},{1,2},{2,3},{3,4},{4,5},{5,6},{6,7},{7,8},{8,9},{9,10... | collective-permute-start | bytes 137096 | tf_op jit(solution)/shard_map/ppermute | solution.py:712
  29.5 5.7 %collective-permute-start.7 = (f32[17,3,336]{2,1,0:T(4,128)S(1)}, f32[17,3,336]{2,1,0:T(4,128)S(1)}, u32[]{:S(2)}, u32[]{:S(2)}) collective-permute-start(f32[17,3,336]{2,1,0:T(4,128)S(1)} %get-tuple-element.34.refs_3_), channel_id=1, source_target_pairs={{1,0},{2,1},{3,2},{4,3},{5,4},{6,5},{7,6},{8,7},{9,8},{10,9},{11,1... | collective-permute-start | bytes 205640 | tf_op jit(solution)/shard_map/ppermute | solution.py:712
  35.2 46.2 %copy-start = (f32[352,512]{1,0:T(8,128)S(1)}, f32[352,512]{1,0:T(8,128)}, u32[]{:S(2)}) copy-start(f32[352,512]{1,0:T(8,128)} %constant.14.clone.refs_1_.refs_3_) | copy-start | bytes 2162692

commit v2 on v1

--- a/solution.py
+++ b/solution.py
@@ -162,6 +162,15 @@
                 places.append(self.put(self.rows, 0, part))
         return tuple(places)
 
+    def add_stacked(self, matrix):
+        high = np.asarray(matrix).astype(ml_dtypes.bfloat16)
+        low = (matrix - high.astype(np.float64)).astype(ml_dtypes.bfloat16)
+        stacked = np.concatenate([high, high, low], axis=1)
+        return tuple(
+            self.put(self.rows, 0, stacked[:, start : start + self.width])
+            for start in range(0, stacked.shape[1], self.width)
+        )
+
     def array(self, dtype, rows=0):
         whole = np.zeros((max(self.rows, rows), self.width), dtype)
         for row, lane, matrix in self.blocks:
@@ -189,7 +198,22 @@
     def mul(a, b):
         return jnp.dot(a, b, preferred_element_type=jnp.float32)
 
+    if left[0].shape[1] % 128 == 0:
+        return mul(
+            jnp.concatenate([left[0], left[0], left[1]], axis=1),
+            jnp.concatenate([right[0], right[1], right[0]], axis=0),
+        )
     return mul(left[0], right[0]) + (mul(left[0], right[1]) + mul(left[1], right[0]))
+
+
+def dot_stacked(tables, right):
+    stacked = jnp.concatenate([right[0], right[1], right[0]], axis=0)
+    total, start = (None, 0)
+    for table in tables:
+        stop = start + table.shape[1]
+        part = jnp.dot(table, stacked[start:stop], preferred_element_type=jnp.float32)
+        total, start = (part if total is None else total + part, stop)
+    return total
 
 
 def dot32(left, right):
@@ -238,12 +262,14 @@
         back_y = np.zeros((16, 20))
         back_y[:14] = back
         ahead_x = pick(ahead, range(20), X_RING, 0, 2)
-        self.ahead_own = smoother.add(np.kron(ahead_x, pick(ahead, range(20), OWN, 0, 2)))
+        self.ahead_own = smoother.add_stacked(np.kron(ahead_x, pick(ahead, range(20), OWN, 0, 2)))
         ahead_edge = pick(ahead, range(20), Y_RING[16:], 0, 2)
         ahead_edge[:, 3] = -ahead[:, 2]
         ahead_edge[:, 4] = -(ahead[:, 9:16] @ stiffness[:7, 7])
-        self.ahead_edge = smoother.add(np.kron(ahead_x, ahead_edge))
-        self.back_xy = smoother.add(np.kron(back, back_y))
+        edge_table = np.zeros((400, 144))
+        edge_table[:, :136] = np.kron(ahead_x, ahead_edge)
+        self.ahead_edge = smoother.add_stacked(edge_table)
+        self.back_xy = smoother.add_stacked(np.kron(back, back_y))
         all_ahead = forward_table(elements_z, basis)[:, 2 : 2 + nodes_z].T * mask_z[:, None]
         all_back = backward_table(elements_z, basis).T * mask_z[None, :]
         self.ahead_z, self.back_z, self.value_columns = ([], [], [])
@@ -315,9 +341,16 @@
         drop_stiff = (inject @ stiff3)[:, 7:21]
         self.drop_b = second.add(np.kron(drop, padded(drop)))
         across = np.kron(drop_stiff, padded(drop_mass)) + np.kron(drop_mass, padded(drop_stiff))
-        self.drop_x = second.add(
-            -np.concatenate([across, np.kron(drop_mass, padded(drop_mass))])
-        )
+        drop_x = -np.concatenate([across, np.kron(drop_mass, padded(drop_mass))])
+        self.drop_x = second.add(drop_x)
+        whole_back = np.kron(back, back_y)
+        self.drop_modes = []
+        for below_x in (0.0, 1.0):
+            for below_y in (0.0, 1.0):
+                mask = np.ones((14, 16))
+                mask[0] *= below_x
+                mask[:, 0] *= below_y
+                self.drop_modes.append(second.add((drop_x * mask.reshape(1, 224)) @ whole_back))
         drop_z = injection_coefficients(elements_z, points)[:elements_z]
         phi_z = sine_modes(np.arange(elements_z), elements_z)
         masked_z = (drop_z * mask_z[None, :]).T
@@ -331,7 +364,7 @@
         phi_x = sine_modes(np.arange(count_x + 1), count_x)
         phi_y = sine_modes(np.arange(count_y + 1), count_y)
         lam_x, lam_y = (coarse_eigen(count_x), coarse_eigen(count_y))
-        assert elements_z <= 64
+        assert elements_z <= 64 and sides_y <= 16
         eigen_z = coarse_eigen(elements_z)
         eye_x = np.eye(4)
         to_y = np.zeros((sides_y, sides_y, 4, 2, 4, 4))
@@ -357,15 +390,23 @@
                 if 2 * place + i - 1 >= 0:
                     to_x[:, place, i] = phi_x[2 * place + i - 1]
             from_x[place, :3] = phi_x[2 * place : 2 * place + 3]
+        lift = injection_coefficients(2, points)
+        lift_xy = np.zeros((14, 16, 16))
+        for number, (i, j) in enumerate(VERTICES):
+            lift_xy[:, :14, number] = np.outer(lift[i], lift[j])
+        lift_xy = lift_xy.reshape(224, 16)
         self.sent = sent = 4 * sides_y
         self.count_x = count_x
         height = -(-sent // 16) * 16
         places = Pack(512)
         for place in range(sides_y):
-            rows = np.zeros((height + 48, 128))
+            rows = np.zeros((height + 272, 128))
             rows[:sent, :32] = to_y[place].reshape(sent, 32)
             rows[height : height + 32, :sent] = from_y[place].reshape(32, sent)
             rows[height + 32] = eigen_yz[place].ravel()
+            for half_mode in range(2):
+                lanes = slice(64 * half_mode, 64 * half_mode + sent)
+                rows[height + 48 :, lanes] = lift_xy @ from_y[place, half_mode].reshape(16, sent)
             places.add(rows, 3)
         self.height = height
         self.place_x_base = places.rows
@@ -373,21 +414,15 @@
             rows = np.zeros((16, 128))
             rows[:, :count_x] = from_x[place]
             places.add(rows, 3)
-        lift = injection_coefficients(2, points)
-        lift_xy = np.zeros((14, 16, 16))
-        for number, (i, j) in enumerate(VERTICES):
-            lift_xy[:, :14, number] = np.outer(lift[i], lift[j])
         lift_z, back_phi = (np.zeros((128, nodes_z)), np.zeros((128, elements_z)))
         for base in (0, 64):
             lift_z[base : base + elements_z] = phi_z.T @ drop_z * mask_z[None, :]
             back_phi[base : base + elements_z] = phi_z.T
-        late = Pack(512)
+        self.lift_z = second.add(lift_z)
+        self.phi_z = second.add(back_phi)
+        late = Pack(256)
         self.to_modes_x = late.put(0, 0, to_x.reshape(count_x, 4 * sides_x))
-        self.lift_xy = late.put(0, 256, lift_xy.reshape(224, 16))
-        self.eigen_x = late.put(0, 384, lam_x[:, None])
-        self.lift_z = late.put(224, 0, lift_z)
-        self.phi_z = late.put(224, 384, back_phi)
-
+        self.eigen_x = late.put(0, 128, lam_x[:, None])
         self.late = late.array(np.float32)
         self.smoother_rows, self.second_rows = (smoother.rows, second.rows)
         self.places_base = smoother.rows + second.rows
@@ -400,6 +435,10 @@
         )
 
 
+def here():
+    return (lax.axis_index("gx"), lax.axis_index("gy"))
+
+
 def sides_of(places, sides):
     flags = []
     for axis in range(2):
@@ -435,17 +474,20 @@
     )
 
 
-def schwarz(modes, edge, tables, smoother):
+def schwarz(modes, edge, inverse, tables, smoother):
     cut = tables.cut
-    edge = split(edge.reshape(136, edge.shape[2]))
-    modes = modes + dot3(parts(smoother, tables.ahead_edge), edge)
-    rows = whole(smoother, tables.value_rows)
+    nodes_z = edge.shape[2]
+    edge = jnp.concatenate(
+        [edge.reshape(136, nodes_z), jnp.zeros((8, nodes_z), jnp.float32)], axis=0
+    )
+    modes = modes + dot_stacked(parts(smoother, tables.ahead_edge), split(edge))
     halves = []
     for number, block in enumerate((modes[:, : tables.first], modes[:, cut:])):
         block = dot3(split(block), parts(smoother, tables.ahead_z[number]))
-        block = block / (rows + whole(smoother, tables.value_columns[number]))
+        block = block * inverse[:, 256 * number : 256 * number + 256]
         halves.append(dot3(split(block), parts(smoother, tables.back_z[number])))
-    return dot3(parts(smoother, tables.back_xy), split(join_z(*halves, cut)))
+    lines = split(join_z(*halves, cut))
+    return (lines, dot_stacked(parts(smoother, tables.back_xy), lines))
 
 
 class Shape(tuple):
@@ -456,7 +498,9 @@
     dtype = jnp.bfloat16
 
 
-def kernel_call(body, inputs, outputs, scratch=(), spaces={}, flops=0, moved=0, room=4):
+def kernel_call(
+    body, inputs, outputs, scratch=(), spaces={}, to=pltpu.VMEM, flops=0, moved=0, room=4
+):
     def kernel(*refs):
         last = len(inputs) + len(outputs)
         body(refs[: len(inputs)], refs[len(inputs) : last], refs[last:])
@@ -468,7 +512,7 @@
             pl.BlockSpec(memory_space=spaces.get(number, pltpu.VMEM))
             for number in range(len(inputs))
         ],
-        out_specs=[pl.BlockSpec(memory_space=pltpu.VMEM) for _ in outputs],
+        out_specs=[pl.BlockSpec(memory_space=to) for _ in outputs],
         scratch_shapes=list(scratch),
         compiler_params=pltpu.CompilerParams(vmem_limit_bytes=room * 1024 * 1024),
         cost_estimate=pl.CostEstimate(flops=flops, bytes_accessed=moved, transcendentals=0),
@@ -495,9 +539,10 @@
 
 def load_second(tables):
     def body(ins, outs, scratch):
-        early, places, _ = ins
+        early, _ = ins
+        places = here()
         base = tables.smoother_rows
-        size = tables.height + 48
+        size = tables.height + 272
         row_y = pl.multiple_of(tables.places_base + size * places[1], 16)
         row_x = pl.multiple_of(tables.places_base + tables.place_x_base + 16 * places[0], 16)
         run_copies(
@@ -512,67 +557,103 @@
     return body
 
 
+def by_partner(first, second, act):
+    even = lax.rem(here()[0], 2) == 0
+    pl.when(even)(lambda: act(first, second))
+    pl.when(jnp.logical_not(even))(lambda: act(second, first))
+
+
 def first_x_rows(ins, outs, scratch):
-    outs[0][...] = ins[0][...]
-    outs[1][...] = ins[0][0:2]
-    outs[2][...] = ins[0][13:14]
+    (own,) = ins
+    outs[0][...] = own[...]
+
+    def write(low, high):
+        low[...] = own[0:2]
+        high[...] = own[12:14]
+
+    by_partner(outs[1], outs[2], write)
 
 
 def first_y_rows(ins, outs, scratch):
-    own, x_low, x_high, _ = ins
-    for out, rows in zip(outs, (slice(0, 2), slice(13, 14))):
+    own, first, second, _ = ins
+    blocks = tuple(zip(outs, (slice(0, 2), slice(13, 14))))
+    for out, rows in blocks:
         out[0:14] = own[:, rows]
-        out[14:16] = x_high[:, rows]
-        out[16:17] = x_low[:, rows]
+
+    def write(low, high):
+        for out, rows in blocks:
+            out[14:16] = high[:, rows]
+            out[16:17] = low[1:2, rows]
+
+    by_partner(first, second, write)
 
 
 def own_modes(tables, sides):
     def body(ins, outs, scratch):
-        places, own, x_low, x_high, smoother = ins
+        own, first, second, smoother = ins
         (line,) = scratch
         nodes_z = own.shape[2]
         line[:, 14:16] = jnp.zeros((17, 2, nodes_z), jnp.float32)
         line[0:14, 0:14] = own[...]
-        line[14:16, 0:14] = x_high[...]
-        line[16:17, 0:14] = x_low[...]
-        masked = line[...] * line_mask(sides_of(places, sides))
+
+        def write(low, high):
+            line[14:16, 0:14] = high[...]
+            line[16:17, 0:14] = low[1:2]
+
+        by_partner(first, second, write)
+        masked = line[...] * line_mask(sides_of(here(), sides))
         outs[0][...] = masked
         rows = split(masked.reshape(272, nodes_z))
-        outs[1][...] = dot3(parts(smoother, tables.ahead_own), rows)
+        outs[1][...] = dot_stacked(parts(smoother, tables.ahead_own), rows)
+        rows = whole(smoother, tables.value_rows)
+        for number, columns in enumerate(tables.value_columns):
+            outs[2][:, 256 * number : 256 * number + 256] = 1.0 / (rows + whole(smoother, columns))
 
     return body
 
 
 def first_sweep(tables, sides):
     def body(ins, outs, scratch):
-        places, modes, y_low, y_high, smoother = ins
-        flags = sides_of(places, sides)
+        modes, y_low, y_high, inverse, smoother = ins
+        flags = sides_of(here(), sides)
         nodes_z = modes.shape[1]
         edge = outs[1]
         edge[:, 0:2] = y_high[...]
         edge[:, 2:3] = y_low[...]
         edge[:, 3:8] = jnp.zeros((17, 5, nodes_z), jnp.float32)
         edge[...] = edge[...] * edge_mask(flags)
-        result = schwarz(modes[...], edge[...], tables, smoother)
+        _, result = schwarz(modes[...], edge[...], inverse, tables, smoother)
         result = result.reshape(14, 16, nodes_z) * (own_mask(flags) * (1.0 / theta_cheb))
         result = result[:, :14]
         outs[0][...] = result
         stiffness = tables.stiffness
-        outs[2][0:2] = result[0:2]
-        outs[3][0:1] = result[13:14]
+        sums = []
         for row in range(2):
-            outs[2][2 + row] = sum(float(stiffness[row, j]) * result[j] for j in range(8))
-            outs[3][1 + row] = sum(float(stiffness[7 - row, j]) * result[7 + j] for j in range(7))
+            sums.append(sum(float(stiffness[row, j]) * result[j] for j in range(8)))
+            sums.append(sum(float(stiffness[7 - row, j]) * result[7 + j] for j in range(7)))
+
+        def write(low, high):
+            low[0:2] = result[0:2]
+            low[2], low[3] = (sums[0], sums[2])
+            high[0], high[1], high[2] = (result[13], sums[1], sums[3])
+            high[3] = jnp.zeros_like(result[0])
+
+        by_partner(outs[2], outs[3], write)
 
     return body
 
 
-def fill_lines(line, own, x_low, x_high):
+def fill_lines(line, own, first, second, sides):
+    flags = sides_of(here(), sides)
     line[:, 14:16] = jnp.zeros((21, 2, own.shape[2]), jnp.float32)
     line[0:14, 0:14] = own[...]
-    line[14:16, 0:14] = x_high[0:2]
-    line[16:19, 0:14] = x_low[...]
-    line[19:21, 0:14] = x_high[2:4]
+
+    def write(low, high):
+        line[14:16, 0:14] = high[0:2] * flags[1]
+        line[16:19, 0:14] = low[0:3] * flags[0]
+        line[19:21, 0:14] = high[2:4] * flags[1]
+
+    by_partner(first, second, write)
 
 
 def apply_z(rows, tables, second):
@@ -583,12 +664,12 @@
     )
 
 
-def edge_rows(tables):
+def edge_rows(tables, sides):
     def body(ins, outs, scratch):
-        own, x_low, x_high, second = ins
+        own, x_first, x_second, second = ins
         line, edge, total = scratch
         nodes_z = own.shape[2]
-        fill_lines(line, own, x_low, x_high)
+        fill_lines(line, own, x_first, x_second, sides)
         edge[...] = jnp.zeros((21, 8, nodes_z), jnp.float32)
         edge[:, 0:2] = line[:, 0:2]
         edge[:, 3:4] = line[:, 13:14]
@@ -608,13 +689,13 @@
     return body
 
 
-def own_rows(tables, sides):
+def own_rows(tables, sides, scale_old):
     def body(ins, outs, scratch):
-        own, x_low, x_high, second, places, source, smoother = ins
+        own, x_first, x_second, second, source, smoother = ins
         line, total = scratch
         modes, from_b = outs
         nodes_z = own.shape[2]
-        fill_lines(line, own, x_low, x_high)
+        fill_lines(line, own, x_first, x_second, sides)
         for number, place in enumerate(tables.own_x):
             rows = line[:, 8 * number : 8 * number + 8].reshape(168, nodes_z)
             part = dot3(parts(second, place), split(rows))
@@ -626,20 +707,23 @@
         along = apply_z(line[0:17].reshape(272, nodes_z), tables, second)
         applied = total[...].reshape(272, nodes_z) * whole(second, tables.mass_z)
         applied = applied + whole(second, tables.mass_own) * along
-        remain = (source[...] - applied.reshape(17, 16, nodes_z)) * line_mask(sides_of(places, sides))
-        modes[...] = dot3(parts(smoother, tables.ahead_own), split(remain.reshape(272, nodes_z)))
+        remain = (source[...] - applied.reshape(17, 16, nodes_z)) * line_mask(sides_of(here(), sides))
+        remain = split(remain.reshape(272, nodes_z))
+        modes[...] = dot_stacked(parts(smoother, tables.ahead_own), remain)
         rows = source[0:14].reshape(224, nodes_z)
-        from_b[...] = dot3(parts(second, tables.drop_b), split(rows))
+        from_b[0:16] = dot3(parts(second, tables.drop_b), split(rows))
+        rows = (1.0 + scale_old) * line[0:14].reshape(224, nodes_z)
+        from_b[16:48] = dot3(parts(second, tables.drop_x), split(rows))
 
     return body
 
 
 def second_sweep(tables, sides, scale_old, scale_new):
     def body(ins, outs, scratch):
-        places, own, modes, to_low, to_high, y_low, y_high, source, from_b = ins[:9]
-        smoother, second, place_y = ins[9:]
-        edge, update = scratch
-        flags = sides_of(places, sides)
+        own, modes, to_low, to_high, y_low, y_high, source, from_b = ins[:8]
+        inverse, smoother, second, place_y = ins[8:]
+        (edge,) = scratch
+        flags = sides_of(here(), sides)
         nodes_z = own.shape[2]
         stiffness = tables.stiffness
         above = y_high[:, 2:3]
@@ -651,18 +735,25 @@
         edge[:, 3:4] = y_low[:, 1:2]
         edge[:, 4:5] = above
         edge[:, 5:8] = jnp.zeros((17, 3, nodes_z), jnp.float32)
-        result = schwarz(modes[...], edge[...] * edge_mask(flags), tables, smoother)
-        update[...] = result.reshape(14, 16, nodes_z) * (own_mask(flags) * scale_new)
-        update[:, 0:14] += (1.0 + scale_old) * own[...]
-        outs[0][...] = update[:, 0:14]
-        from_x = dot3(parts(second, tables.drop_x), split(update[...].reshape(224, nodes_z)))
-        both = jnp.concatenate([from_b[...], from_x], axis=0)
+        lines, result = schwarz(modes[...], edge[...] * edge_mask(flags), inverse, tables, smoother)
+        below_x, _, below_y, _ = flags
+        number = jnp.where(below_x > 0.0, 2, 0) + jnp.where(below_y > 0.0, 1, 0)
+        (rows, lanes), (more, _) = tables.drop_modes[0]
+        step = tables.drop_modes[1][0][0].start - rows.start
+        drop = tuple(
+            second[pl.ds(pl.multiple_of(part.start + step * number, 16), 32), lanes]
+            for part in (rows, more)
+        )
+        from_x = scale_new * dot3(drop, lines)
+        both = jnp.concatenate([from_b[0:16], from_b[16:48] + from_x], axis=0)
+        result = result.reshape(14, 16, nodes_z) * (own_mask(flags) * scale_new)
+        outs[0][...] = (1.0 + scale_old) * own[...] + result[:, 0:14]
         modes = dot3(split(both), parts(second, tables.modes_z))
         modes = modes[0:16, 0:128] + modes[16:32, 128:256] + modes[32:48, 256:384]
         left = lax.broadcasted_iota(jnp.int32, (16, 128), 1) < 64
         modes = jnp.concatenate([jnp.where(left, modes, 0.0), jnp.where(left, 0.0, modes)], axis=0)
-        to_modes_y = whole(place_y, tables.place_parts, slice(0, tables.sent))[:, 0:32]
-        outs[1][...] = dot32(to_modes_y, modes).reshape(outs[1].shape)
+        to_modes_y = [part[0 : tables.sent, 0:32] for part in parts(place_y, tables.place_parts[:2])]
+        outs[1][...] = dot3(to_modes_y, split(modes)).reshape(outs[1].shape)
 
     return body
 
@@ -686,44 +777,71 @@
 
 def finish(tables, sides):
     def body(ins, outs, scratch):
-        places, arrived, approx, late, place_y = ins
+        arrived, approx, second, place_y = ins
+        sums, vertices_out, semaphores = scratch
         nodes_z = approx.shape[2]
-        rows = slice(tables.height, tables.height + 32)
-        from_modes_y = whole(place_y, tables.place_parts, rows)[:, 0 : tables.sent]
-        vertices = dot3(split(from_modes_y), split(arrived[...].reshape(-1, 128)))
+        rows = arrived[...].reshape(-1, 128)
+        left = lax.broadcasted_iota(jnp.int32, rows.shape, 1) < 64
+        lines = jnp.concatenate([jnp.where(left, rows, 0.0), jnp.where(left, 0.0, rows)], axis=0)
+        if tables.sent < 64:
+            empty = jnp.zeros((64 - tables.sent, 128), jnp.float32)
+            lines = jnp.concatenate(
+                [lines[: tables.sent], empty, lines[tables.sent :], empty], axis=0
+            )
+        lines = dot3(split(lines), parts(second, tables.lift_z))
+        back = slice(tables.height, tables.height + 32)
+        back = [place_y[back, lanes][:, 0 : tables.sent] for _, lanes in tables.place_parts[:2]]
+        vertices = dot3(back, split(rows))
         left = lax.broadcasted_iota(jnp.int32, (16, 128), 1) < 64
         vertices = split(jnp.where(left, vertices[0:16], vertices[16:32]))
-        coarse = dot3(vertices, split(late[tables.phi_z]))
-        outs[1][0] = coarse[0:2]
-        outs[1][1] = coarse[2:4]
-        lines = dot3(vertices, split(late[tables.lift_z]))
-        fine = dot3(split(late[tables.lift_xy]), split(lines))
-        fine = fine.reshape(14, 16, nodes_z) * own_mask(sides_of(places, sides))
-        outs[0][...] = approx[...] + fine[:, :14]
+        coarse = dot3(vertices, parts(second, tables.phi_z))
+        vertices_out[0] = coarse[0:2]
+        vertices_out[1] = coarse[2:4]
+        copies = [pltpu.make_async_copy(vertices_out, outs[1], semaphores.at[2])]
+        copies[0].start()
+        lines = split(lines)
+        mask = own_mask(sides_of(here(), sides))
+        base = tables.height + 48
+        for number, (low, high) in enumerate(((0, 7), (7, 14))):
+            lift = slice(base + 16 * low, base + 16 * high)
+            lift = tuple(place_y[lift, lanes] for _, lanes in tables.place_parts[:2])
+            fine = dot3(lift, lines).reshape(high - low, 16, nodes_z) * mask[low:high]
+            sums[low:high] = approx[low:high] + fine[:, :14]
+            copies.append(
+                pltpu.make_async_copy(
+                    sums.at[low:high], outs[0].at[low:high], semaphores.at[number]
+                )
+            )
+            copies[-1].start()
+        for copy in copies:
+            copy.wait()
 
     return body
 
 
-def shift(block, axis, distance):
-    count = lax.axis_size(axis)
-    route = [((i - distance) % count, i) for i in range(count)]
-    if axis == "gx":
-        route = [(i, j) for i, j in route if j - i == distance]
-    return lax.ppermute(block, axis, route)
+def shift_y(block, distance):
+    count = lax.axis_size("gy")
+    return lax.ppermute(block, "gy", [((i - distance) % count, i) for i in range(count)])
+
+
+def swap_x(first, second):
+    count = lax.axis_size("gx")
+    assert count % 2 == 0
+    across = [(i, (i + 1 if i % 2 else i - 1) % count) for i in range(count)]
+    within = [(i, i ^ 1) for i in range(count)]
+    return (lax.ppermute(first, "gx", across), lax.ppermute(second, "gx", within))
 
 
 def per_device(residual_in):
     nodes_x, nodes_y, nodes_z = residual_in.shape
     assert nodes_x == 14 and nodes_y == 14 and nodes_z % 14 == 0
     sides = (lax.axis_size("gx"), lax.axis_size("gy"))
-    places = jnp.stack([lax.axis_index("gx"), lax.axis_index("gy")]).astype(jnp.int32)
     elements_z = nodes_z // 7
     tables = Tables(elements_z, 2 * sides[0], 2 * sides[1])
     early, late = (jnp.asarray(tables.early), jnp.asarray(tables.late))
     sigma_ratio = theta_cheb / delta_cheb
     rho_now = 1.0 / sigma_ratio
     rho_next = 1.0 / (2.0 * sigma_ratio - rho_now)
-    scalars = {0: pltpu.SMEM}
 
     def block(*shape):
         return Shape(shape + (nodes_z,))
@@ -731,10 +849,12 @@
     def scratch(*shape):
         return pltpu.VMEM(shape + (nodes_z,), jnp.float32)
 
-    own, to_low, to_high = kernel_call(
-        first_x_rows, [residual_in], [block(14, 14), block(2, 14), block(1, 14)]
-    )
-    x_low, x_high = (shift(to_high, "gx", 1), shift(to_low, "gx", -1))
+    own, to_first, to_second = kernel_call(
+        first_x_rows,
+        [residual_in],
+        [block(14, 14), block(2, 14), block(2, 14)],
+    )
+    x_first, x_second = swap_x(to_first, to_second)
     (smoother,) = kernel_call(
         load_smoother(tables),
         [early],
@@ -745,46 +865,45 @@
         room=LOADER_ROOM,
     )
     to_low, to_high = kernel_call(
-        first_y_rows, [own, x_low, x_high, smoother], [block(17, 2), block(17, 1)]
-    )
-    y_low, y_high = (shift(to_high, "gy", 1), shift(to_low, "gy", -1))
-    source, modes = kernel_call(
+        first_y_rows,
+        [own, x_first, x_second, smoother],
+        [block(17, 2), block(17, 1)],
+    )
+    y_low, y_high = (shift_y(to_high, 1), shift_y(to_low, -1))
+    source, modes, inverse = kernel_call(
         own_modes(tables, sides),
-        [places, own, x_low, x_high, smoother],
-        [block(17, 16), block(400)],
+        [own, x_first, x_second, smoother],
+        [block(17, 16), block(400), Shape((400, 512))],
         [scratch(17, 16)],
-        scalars,
         flops=500_000_000,
         moved=2_000_000,
         room=8,
     )
-    direction, edge, to_low, to_high = kernel_call(
+    direction, edge, to_first, to_second = kernel_call(
         first_sweep(tables, sides),
-        [places, modes, y_low, y_high, smoother],
-        [block(14, 14), block(17, 8), block(4, 14), block(3, 14)],
-        (),
-        scalars,
+        [modes, y_low, y_high, inverse, smoother],
+        [block(14, 14), block(17, 8), block(4, 14), block(4, 14)],
         flops=2_000_000_000,
         moved=4_000_000,
         room=8,
     )
-    x_low, x_high = (shift(to_high, "gx", 1), shift(to_low, "gx", -1))
+    x_first, x_second = swap_x(to_first, to_second)
     second, place_y, place_x = kernel_call(
         load_second(tables),
-        [early, places, to_low],
+        [early, to_first],
         [
             HalfShape((tables.second_rows, 512)),
-            HalfShape((tables.height + 48, 512)),
+            HalfShape((tables.height + 272, 512)),
             HalfShape((16, 512)),
         ],
         [pltpu.SemaphoreType.DMA((3,))],
-        {0: pl.ANY, 1: pltpu.SMEM},
+        {0: pl.ANY},
         moved=6_000_000,
         room=LOADER_ROOM,
     )
-    lines = [direction, x_low, x_high, second]
+    lines = [direction, x_first, x_second, second]
     to_low, to_high = kernel_call(
-        edge_rows(tables),
+        edge_rows(tables, sides),
         lines,
         [block(17, 3), block(17, 2)],
         [scratch(21, 16), scratch(21, 8), scratch(17, 8)],
@@ -792,24 +911,22 @@
         moved=2_000_000,
         room=8,
     )
-    y_low, y_high = (shift(to_high, "gy", 1), shift(to_low, "gy", -1))
+    y_low, y_high = (shift_y(to_high, 1), shift_y(to_low, -1))
     modes, from_b = kernel_call(
-        own_rows(tables, sides),
-        lines + [places, source, smoother],
-        [block(400), block(16)],
+        own_rows(tables, sides, rho_next * rho_now),
+        lines + [source, smoother],
+        [block(400), block(48)],
         [scratch(21, 16), scratch(17, 16)],
-        {4: pltpu.SMEM},
         flops=1_500_000_000,
         moved=3_000_000,
         room=8,
     )
     approx, outgoing = kernel_call(
         second_sweep(tables, sides, rho_next * rho_now, 2.0 * rho_next / delta_cheb),
-        [places, direction, modes, to_low, to_high, y_low, y_high, edge, from_b]
-        + [smoother, second, place_y],
+        [direction, modes, to_low, to_high, y_low, y_high, edge, from_b]
+        + [inverse, smoother, second, place_y],
         [block(14, 14), Shape((sides[1], 4, 128))],
-        [scratch(17, 8), scratch(14, 16)],
-        scalars,
+        [scratch(17, 8)],
         flops=3_000_000_000,
         moved=6_000_000,
         room=8,
@@ -823,10 +940,14 @@
     arrived = lax.all_to_all(outgoing, "gy", 0, 0, tiled=True)
     correction, coarse = kernel_call(
         finish(tables, sides),
-        [places, arrived, approx, late, place_y],
+        [arrived, approx, second, place_y],
         [block(14, 14), Shape((2, 2, elements_z))],
-        (),
-        scalars,
+        [
+            scratch(14, 14),
+            pltpu.VMEM((2, 2, elements_z), jnp.float32),
+            pltpu.SemaphoreType.DMA((3,)),
+        ],
+        to=pl.ANY,
     )
     return (correction, coarse)
 

time: 95.8 us -> 88.3 us (0.922)
  blocking collectives: 54.6 us -> 44.1 us
  Pallas kernels: 16.7 us -> 12.7 us
  starting transfers between devices: 19.9 us -> 23.9 us
  waiting for transfers between devices: 2.35 us -> 5.53 us
    all_to_all x1, blocking collectives: 26.3 us -> 14.8 us  [per_device(): arrived = lax.all_to_all(outgoing, 'gx', 0, 0, tiled=True)]
    ppermute x8, starting transfers between devices: 19.9 us -> 23.9 us  [the longest x2 11.2 us: swap_x(): lax.ppermute(first, 'gx', across)]
    pallas_call x12, Pallas kernels: 16.7 us -> 12.7 us  [kernel_call(): pl.pallas_call(kernel, out_shape=[jax.ShapeDtypeStruct(shape, shape.dtype...]
    ppermute x8, waiting for transfers between devices: 2.35 us -> 5.53 us  [the longest x4 2.9 us: shift_y(): lax.ppermute(block, 'gy', [((i - distance) % count, i) for i in range(cou...]
  transfers between devices with their start and end apart: 8 -> 8, of which waited for: 2 -> 4; matrix products, arithmetic and copies ran while one was open for 0% -> 0% of each run, Pallas kernels for 8% -> 7%
where the time goes in v2:
time: 88.3 us; the launch traced here: 87.9 us
  blocking collectives  44.1 us (50%)
  starting transfers between devices  23.9 us (27%)
  Pallas kernels  12.7 us (14%)
  waiting for transfers between devices  5.53 us (6%)
  local copies, waits for them, and re-layouts  0.98 us (1%)
    all_to_all x2, blocking collectives, per_device(): arrived = lax.all_to_all(outgoing, 'gy', 0, 0, tiled=True)  29.3 us
    all_to_all x1, blocking collectives, per_device(): arrived = lax.all_to_all(outgoing, 'gx', 0, 0, tiled=True)  14.8 us
    pallas_call x12, Pallas kernels, kernel_call(): pl.pallas_call(kernel, out_shape=[jax.ShapeDtypeStruct(shape, shape.dtype...  12.7 us
    ppermute x2, starting transfers between devices, swap_x(): lax.ppermute(first, 'gx', across)  11.2 us
    ppermute x4, starting transfers between devices, shift_y(): lax.ppermute(block, 'gy', [((i - distance) % count, i) for i in range(cou...  8.9 us
    ppermute x2, starting transfers between devices, swap_x(): lax.ppermute(second, 'gx', within)  3.84 us
    ppermute x4, waiting for transfers between devices, shift_y(): lax.ppermute(block, 'gy', [((i - distance) % count, i) for i in range(cou...  2.9 us
  transfers between devices with their start and end apart: 8, of which 4 were waited for; matrix products, arithmetic and copies ran while one was open for 0% of the time, Pallas kernels for 7%

profile of v2, /device:TPU:1, one launch (start us, length us, event | category | flops | bytes accessed | tf_op | source)
XLA Modules:
  0.0 87.9 jit_solution(12052907724780047989)
XLA Ops:
  0.6 0.0 copy-start
  0.6 1.0 %copy-done = f32[14,14,336]{2,1,0:T(8,128)S(1)} copy-done((f32[14,14,336]{2,1,0:T(8,128)S(1)}, f32[14,14,336]{2,1,0:T(8,128)}, u32[]{:S(2)}) %copy-start) | copy-done | bytes 263448
  1.6 8.1 %collective-permute-start = (f32[2,14,336]{2,1,0:T(8,128)S(1)}, f32[2,14,336]{2,1,0:T(8,128)S(1)}, u32[]{:S(2)}, u32[]{:S(2)}) collective-permute-start(f32[2,14,336]{2,1,0:T(8,128)S(1)} %get-tuple-element.24), channel_id=1, source_target_pairs={{0,496},{16,32},{32,16},{48,64},{64,48},{80,96},{96,80},{112,128},... | collective-permute-start | bytes 112904 | tf_op jit(solution)/shard_map/ppermute | solution.py:832
  9.8 1.9 %collective-permute-start.1 = (f32[2,14,336]{2,1,0:T(8,128)S(1)}, f32[2,14,336]{2,1,0:T(8,128)S(1)}, u32[]{:S(2)}, u32[]{:S(2)}) collective-permute-start(f32[2,14,336]{2,1,0:T(8,128)S(1)} %get-tuple-element.25), channel_id=1, source_target_pairs={{0,16},{16,0},{32,48},{48,32},{64,80},{80,64},{96,112},{112,96},{1... | collective-permute-start | bytes 112904 | tf_op jit(solution)/shard_map/ppermute | solution.py:832
  11.7 2.0 %shard_map.51.refs_3_.refs_4_.refs_5_.refs_9_ = bf16[3344,512]{1,0:T(8,128)(2,1)S(1)} custom-call(bf16[20480,512]{1,0:T(8,128)(2,1)} %constant.4.clone.refs_0_), custom_call_target="tpu_custom_call" | custom-call | bytes 6000000 | tf_op jit(solution)/shard_map/pallas_call | solution.py:508
  13.7 0.0 collective-permute-done.refs_1_
  13.7 0.9 %collective-permute-done.1.refs_2_ = f32[2,14,336]{2,1,0:T(8,128)S(1)} collective-permute-done((f32[2,14,336]{2,1,0:T(8,128)S(1)}, f32[2,14,336]{2,1,0:T(8,128)S(1)}, u32[]{:S(2)}, u32[]{:S(2)}) %collective-permute-start.1) | collective-permute-done | bytes 37664 | tf_op jit(solution)/shard_map/ppermute | solution.py:832
  14.7 4.1 %collective-permute-start.2 = (f32[17,1,336]{2,1,0:T(1,128)S(1)}, f32[17,1,336]{2,1,0:T(1,128)S(1)}, u32[]{:S(2)}, u32[]{:S(2)}) collective-permute-start(f32[17,1,336]{2,1,0:T(1,128)S(1)} %get-tuple-element.27), channel_id=1, source_target_pairs={{15,0},{0,1},{1,2},{2,3},{3,4},{4,5},{5,6},{6,7},{7,8},{8,9},{9,10... | collective-permute-start | bytes 68552 | tf_op jit(solution)/shard_map/ppermute | solution.py:824
  18.7 0.0 collective-permute-start.3
  18.8 0.6 shard_map.52
  19.4 0.3 collective-permute-done.2.refs_1_
  19.7 2.6 %collective-permute-done.3.refs_2_ = f32[17,2,336]{2,1,0:T(2,128)S(1)} collective-permute-done((f32[17,2,336]{2,1,0:T(2,128)S(1)}, f32[17,2,336]{2,1,0:T(2,128)S(1)}, u32[]{:S(2)}, u32[]{:S(2)}) %collective-permute-start.3) | collective-permute-done | bytes 45728 | tf_op jit(solution)/shard_map/ppermute | solution.py:824
  22.3 1.8 %shard_map.54 = (f32[14,14,336]{2,1,0:T(8,128)S(1)}, f32[17,8,336]{2,1,0:T(8,128)S(1)}, f32[4,14,336]{2,1,0:T(8,128)S(1)}, f32[4,14,336]{2,1,0:T(8,128)S(1)}) custom-call(f32[400,336]{1,0:T(8,128)S(1)} %get-tuple-element.26.refs_0_, f32[17,1,336]{2,1,0:T(1,128)S(1)} %collective-permute-done.2.refs_1_, f32[17,2,336]{2,1,0:T(2,128)S(1)} %collective-permute-done.3.refs_2_, ...), custom_call_target="tpu_custom_call" | custom-call | flops 2000000000 | bytes 4000000 | tf_op jit(solution)/shard_map/pallas_call | solution.py:508
  24.1 3.0 %collective-permute-start.4 = (f32[4,14,336]{2,1,0:T(8,128)S(1)}, f32[4,14,336]{2,1,0:T(8,128)S(1)}, u32[]{:S(2)}, u32[]{:S(2)}) collective-permute-start(f32[4,14,336]{2,1,0:T(8,128)S(1)} %get-tuple-element.31.refs_1_), channel_id=1, source_target_pairs={{0,496},{16,32},{32,16},{48,64},{64,48},{80,96},{96,80},{112,128},... | collective-permute-start | bytes 225800 | tf_op jit(solution)/shard_map/ppermute | solution.py:832
  27.2 1.9 %collective-permute-start.5 = (f32[4,14,336]{2,1,0:T(8,128)S(1)}, f32[4,14,336]{2,1,0:T(8,128)S(1)}, u32[]{:S(2)}, u32[]{:S(2)}) collective-permute-start(f32[4,14,336]{2,1,0:T(8,128)S(1)} %get-tuple-element.32), channel_id=1, source_target_pairs={{0,16},{16,0},{32,48},{48,32},{64,80},{80,64},{96,112},{112,96},{1... | collective-permute-start | bytes 225800 | tf_op jit(solution)/shard_map/ppermute | solution.py:832
  29.1 2.0 %shard_map.55 = (bf16[3136,512]{1,0:T(8,128)(2,1)S(1)}, bf16[336,512]{1,0:T(8,128)(2,1)S(1)}, bf16[16,512]{1,0:T(8,128)(2,1)S(1)}) custom-call(bf16[20480,512]{1,0:T(8,128)(2,1)} %constant.4.clone.refs_0_, f32[4,14,336]{2,1,0:T(8,128)S(1)} %get-tuple-element.31.refs_1_), custom_call_target="tpu_custom_call" | custom-call | bytes 6000000 | tf_op jit(solution)/shard_map/pallas_call | solution.py:508
  31.1 1.7 %collective-permute-done.4.refs_1_ = f32[4,14,336]{2,1,0:T(8,128)S(1)} collective-permute-done((f32[4,14,336]{2,1,0:T(8,128)S(1)}, f32[4,14,336]{2,1,0:T(8,128)S(1)}, u32[]{:S(2)}, u32[]{:S(2)}) %collective-permute-start.4) | collective-permute-done | bytes 75296 | tf_op jit(solution)/shard_map/ppermute | solution.py:832
  32.8 0.0 collective-permute-done.5.refs_2_
  32.8 0.7 shard_map.57
  33.5 1.1 %collective-permute-start.6 = (f32[17,2,336]{2,1,0:T(2,128)S(1)}, f32[17,2,336]{2,1,0:T(2,128)S(1)}, u32[]{:S(2)}, u32[]{:S(2)}) collective-permute-start(f32[17,2,336]{2,1,0:T(2,128)S(1)} %get-tuple-element.37.refs_3_), channel_id=1, source_target_pairs={{15,0},{0,1},{1,2},{2,3},{3,4},{4,5},{5,6},{6,7},{7,8},{8,9},{9,10... | collective-permute-start | bytes 137096 | tf_op jit(solution)/shard_map/ppermute | solution.py:824
  34.6 3.7 %collective-permute-start.7 = (f32[17,3,336]{2,1,0:T(4,128)S(1)}, f32[17,3,336]{2,1,0:T(4,128)S(1)}, u32[]{:S(2)}, u32[]{:S(2)}) collective-permute-start(f32[17,3,336]{2,1,0:T(4,128)S(1)} %get-tuple-element.36.refs_2_), channel_id=1, source_target_pairs={{1,0},{2,1},{3,2},{4,3},{5,4},{6,5},{7,6},{8,7},{9,8},{10,9},{11,1... | collective-permute-start | bytes 205640 | tf_op jit(solution)/shard_map/ppermute | solution.py:824
  38.3 1.6 %shard_map.56 = (f32[400,336]{1,0:T(8,128)S(1)}, f32[48,336]{1,0:T(8,128)S(1)}) custom-call(f32[14,14,336]{2,1,0:T(8,128)S(1)} %get-tuple-element.30.refs_0_, f32[4,14,336]{2,1,0:T(8,128)S(1)} %collective-permute-done.4.refs_1_, f32[4,14,336]{2,1,0:T(8,128)S(1)} %collective-permute-done.5.refs_2_, ...), custom_call_target="tpu_custom_call" | custom-call | flops 1500000000 | bytes 3000000 | tf_op jit(solution)/shard_map/pallas_call | solution.py:508
  39.9 0.0 collective-permute-done.6.refs_4_
  39.9 0.0 collective-permute-done.7.refs_5_
  39.9 0.0 copy-start.1
  39.9 2.4 %shard_map.58 = (f32[14,14,336]{2,1,0:T(8,128)S(1)}, f32[16,4,128]{2,1,0:T(4,128)S(1)}) custom-call(f32[14,14,336]{2,1,0:T(8,128)S(1)} %get-tuple-element.30.refs_0_, f32[400,336]{1,0:T(8,128)S(1)} %get-tuple-element.35.refs_1_, f32[17,3,336]{2,1,0:T(4,128)S(1)} %get-tuple-element.36.refs_2_, f32[17,2,336]{2,1,0:T(2,128)S(1)} %get-tuple-element.37.refs_3_, ...), custom_call_target="tpu_custom_call" | custom-call | flops 3000000000 | bytes 6000000 | tf_op jit(solution)/shard_map/pallas_call | solution.py:508
  42.3 17.6 %all_to_all.15.refs_0_ = f32[16,4,128]{2,1,0:T(4,128)S(1)} all-to-all(f32[16,4,128]{2,1,0:T(4,128)S(1)} %get-tuple-element.41), channel_id=1, replica_groups=mesh['gx'=32,'gy'=16] {'gy'}, dimensions={0} | all-to-all | bytes 65536 | tf_op jit(solution)/shard_map/all_to_all | solution.py:934
  59.9 14.8 %all_to_all.16.refs_0_ = f32[32,4,128]{2,1,0:T(4,128)S(1)} all-to-all(f32[32,4,128]{2,1,0:T(4,128)S(1)} %shard_map.59), channel_id=1, replica_groups=mesh['gx'=32,'gy'=16] {'gx'}, dimensions={0} | all-to-all | bytes 131072 | tf_op jit(solution)/shard_map/all_to_all | solution.py:936
  74.7 0.0 copy-done.1
  74.7 0.3 shard_map.60
  75.0 11.7 %all_to_all.17.refs_0_ = f32[16,4,128]{2,1,0:T(4,128)S(1)} all-to-all(f32[16,4,128]{2,1,0:T(4,128)S(1)} %shard_map.60), channel_id=1, replica_groups=mesh['gx'=32,'gy'=16] {'gy'}, dimensions={0} | all-to-all | bytes 65536 | tf_op jit(solution)/shard_map/all_to_all | solution.py:940
  86.8 1.2 %shard_map.61 = (f32[14,14,336]{2,1,0:T(8,128)}, f32[2,2,48]{2,1,0:T(2,128)}) custom-call(f32[16,4,128]{2,1,0:T(4,128)S(1)} %all_to_all.17.refs_0_, f32[14,14,336]{2,1,0:T(8,128)S(1)} %get-tuple-element.43.refs_1_, bf16[3136,512]{1,0:T(8,128)(2,1)S(1)} %get-tuple-element.33.refs_3_.refs_10_.refs_2_, bf16[336,512]{1,0:T(8,128)(2,1)S(1)} %get-tuple-element.40.refs_11_.refs_3_), custom_call_target="tpu_custom_call" | custom-call | tf_op jit(solution)/shard_map/pallas_call | solution.py:508
  (3 shorter events, 0.1 us)
Async XLA Ops:
  0.6 1.0 %copy-start = (f32[14,14,336]{2,1,0:T(8,128)S(1)}, f32[14,14,336]{2,1,0:T(8,128)}, u32[]{:S(2)}) copy-start(f32[14,14,336]{2,1,0:T(8,128)} %refs_0_.3) | copy-start | bytes 790276
  1.6 12.0 %collective-permute-start = (f32[2,14,336]{2,1,0:T(8,128)S(1)}, f32[2,14,336]{2,1,0:T(8,128)S(1)}, u32[]{:S(2)}, u32[]{:S(2)}) collective-permute-start(f32[2,14,336]{2,1,0:T(8,128)S(1)} %get-tuple-element.24), channel_id=1, source_target_pairs={{0,496},{16,32},{32,16},{48,64},{64,48},{80,96},{96,80},{112,128},... | collective-permute-start | bytes 112904 | tf_op jit(solution)/shard_map/ppermute | solution.py:832
  9.8 4.8 %collective-permute-start.1 = (f32[2,14,336]{2,1,0:T(8,128)S(1)}, f32[2,14,336]{2,1,0:T(8,128)S(1)}, u32[]{:S(2)}, u32[]{:S(2)}) collective-permute-start(f32[2,14,336]{2,1,0:T(8,128)S(1)} %get-tuple-element.25), channel_id=1, source_target_pairs={{0,16},{16,0},{32,48},{48,32},{64,80},{80,64},{96,112},{112,96},{1... | collective-permute-start | bytes 112904 | tf_op jit(solution)/shard_map/ppermute | solution.py:832
  14.7 5.1 %collective-permute-start.2 = (f32[17,1,336]{2,1,0:T(1,128)S(1)}, f32[17,1,336]{2,1,0:T(1,128)S(1)}, u32[]{:S(2)}, u32[]{:S(2)}) collective-permute-start(f32[17,1,336]{2,1,0:T(1,128)S(1)} %get-tuple-element.27), channel_id=1, source_target_pairs={{15,0},{0,1},{1,2},{2,3},{3,4},{4,5},{5,6},{6,7},{7,8},{8,9},{9,10... | collective-permute-start | bytes 68552 | tf_op jit(solution)/shard_map/ppermute | solution.py:824
  18.7 3.5 %collective-permute-start.3 = (f32[17,2,336]{2,1,0:T(2,128)S(1)}, f32[17,2,336]{2,1,0:T(2,128)S(1)}, u32[]{:S(2)}, u32[]{:S(2)}) collective-permute-start(f32[17,2,336]{2,1,0:T(2,128)S(1)} %get-tuple-element.28), channel_id=1, source_target_pairs={{1,0},{2,1},{3,2},{4,3},{5,4},{6,5},{7,6},{8,7},{9,8},{10,9},{11,1... | collective-permute-start | bytes 137096 | tf_op jit(solution)/shard_map/ppermute | solution.py:824
  24.1 8.7 %collective-permute-start.4 = (f32[4,14,336]{2,1,0:T(8,128)S(1)}, f32[4,14,336]{2,1,0:T(8,128)S(1)}, u32[]{:S(2)}, u32[]{:S(2)}) collective-permute-start(f32[4,14,336]{2,1,0:T(8,128)S(1)} %get-tuple-element.31.refs_1_), channel_id=1, source_target_pairs={{0,496},{16,32},{32,16},{48,64},{64,48},{80,96},{96,80},{112,128},... | collective-permute-start | bytes 225800 | tf_op jit(solution)/shard_map/ppermute | solution.py:832
  27.2 5.6 %collective-permute-start.5 = (f32[4,14,336]{2,1,0:T(8,128)S(1)}, f32[4,14,336]{2,1,0:T(8,128)S(1)}, u32[]{:S(2)}, u32[]{:S(2)}) collective-permute-start(f32[4,14,336]{2,1,0:T(8,128)S(1)} %get-tuple-element.32), channel_id=1, source_target_pairs={{0,16},{16,0},{32,48},{48,32},{64,80},{80,64},{96,112},{112,96},{1... | collective-permute-start | bytes 225800 | tf_op jit(solution)/shard_map/ppermute | solution.py:832
  33.5 6.4 %collective-permute-start.6 = (f32[17,2,336]{2,1,0:T(2,128)S(1)}, f32[17,2,336]{2,1,0:T(2,128)S(1)}, u32[]{:S(2)}, u32[]{:S(2)}) collective-permute-start(f32[17,2,336]{2,1,0:T(2,128)S(1)} %get-tuple-element.37.refs_3_), channel_id=1, source_target_pairs={{15,0},{0,1},{1,2},{2,3},{3,4},{4,5},{5,6},{6,7},{7,8},{8,9},{9,10... | collective-permute-start | bytes 137096 | tf_op jit(solution)/shard_map/ppermute | solution.py:824
  34.6 5.3 %collective-permute-start.7 = (f32[17,3,336]{2,1,0:T(4,128)S(1)}, f32[17,3,336]{2,1,0:T(4,128)S(1)}, u32[]{:S(2)}, u32[]{:S(2)}) collective-permute-start(f32[17,3,336]{2,1,0:T(4,128)S(1)} %get-tuple-element.36.refs_2_), channel_id=1, source_target_pairs={{1,0},{2,1},{3,2},{4,3},{5,4},{6,5},{7,6},{8,7},{9,8},{10,9},{11,1... | collective-permute-start | bytes 205640 | tf_op jit(solution)/shard_map/ppermute | solution.py:824
  39.9 34.8 %copy-start.1 = (f32[64,256]{1,0:T(8,128)S(1)}, f32[64,256]{1,0:T(8,128)}, u32[]{:S(2)}) copy-start(f32[64,256]{1,0:T(8,128)} %constant.5.clone.refs_1_) | copy-start | bytes 196612
